TPU v7x, 256 devices: a whole 4x4x8 slice. The times are simulated.
256 devices in a mesh: gx: 4 (over y), gy: 8 (over z), gz: 8 (over x, core).
Axes of the slice: x: 4, y: 4, z: 8, core: 2. Of those that a mesh axis runs over, the one named last changes fastest.
Arguments:
- right_side: float32 [16, 32, 64, 1024], P(None, 'gx', 'gy', 'gz'), may hold values from -21 to 21, as said below
- absorption: float32 [32, 64, 1024], P('gx', 'gy', 'gz'), may hold values from 0.25 to 4
- velocity: float32 [3, 32, 64, 1024], P(None, 'gx', 'gy', 'gz'), may hold values from -1 to 1
Outputs:
- solution_field: float32 [16, 32, 64, 1024], P(None, 'gx', 'gy', 'gz')
- residual: float32 [16, 32, 64, 1024], P(None, 'gx', 'gy', 'gz')
Inputs may be any that keep to these rules, and one draw needn't show every extreme that they name: `right_side`: Right-hand sides of order one, scaled from cell to cell.
All inputs are finite; a program needn't handle non-finite values.
Results may differ from a plain program's by a relative error of at most 0.0003.
Values sent between devices are 32-bit elements; how exact they have to be, the bound alone decides.
No kernel may reach another device: no remote copies, remote signals or barrier semaphores. Data moves between devices by JAX's collectives and lax.ppermute only.
A program may use at most 128 MiB of HBM per device.

v0:
```python
import jax
import jax.numpy as jnp
from jax import lax
from jax.experimental import pallas as pl
from jax.experimental.pallas import tpu as pltpu
from jax.sharding import Mesh, PartitionSpec as P

RHS = 16
STEPS = 4
COLS = RHS * (STEPS + 1)
KEEP = RHS * STEPS
FILLS = 4
MAKES = 7
OWN = 8
GRAMS = 16
PAIRS = 8
BLOCK = 4
LOW = RHS * 512
HIGH = LOW + 512
LIMIT = 28 * 1024 * 1024
F32 = jnp.float32
BF16 = jnp.bfloat16


def lanes():
    return lax.broadcasted_iota(jnp.int32, (8, 128), 1)


def rolled(x, amount):
    amount = amount % x.shape[-1]
    return x if amount == 0 else pltpu.roll(x, amount, x.ndim - 1)


def wide(pieces):
    return jnp.concatenate(pieces, axis=0)


FACE_ROWS = RHS * 32 + 4 * 24


def face_at(f, side):
    count = 4 if f < RHS else 3
    start = f * 32 if f < RHS else RHS * 32 + (f - RHS) * 24
    return start, count, (0 if side == 0 else 8 - count)


def pack_own(own, ends, xlow, xhigh, ylow, yhigh):
    group = lanes() // 8
    for x in range(8):
        tiles = [own[f * 64 + x * 8 : f * 64 + x * 8 + 8, :] for f in range(RHS + 4)]
        for part, at in ((tiles[:RHS], 0), (tiles[RHS:], 64)):
            acc = rolled(part[0], 4)
            for i in range(1, len(part)):
                acc = jnp.where(group == i, rolled(part[i], 8 * i + 4), acc)
            ends[at + x * 8 : at + x * 8 + 8, :] = acc
        for f, tile in enumerate(tiles):
            for side, (xout, yout) in enumerate(((xlow, ylow), (xhigh, yhigh))):
                start, count, first = face_at(f, side)
                if first <= x < first + count:
                    xout[start + (x - first) * 8 : start + (x - first) * 8 + 8, :] = tile
                yout[start + x * count : start + x * count + count, :] = tile[first : first + count]


REACH = ((0, 3), (24, 2), (40, 2), (56, 1))


def pack_ends(flags, ends, zprev, znext, slabs, xlow, xhigh):
    low = lanes() % 8 < 4
    zm, zp = flags[4], flags[5]
    for j in range(4):
        for x in range(8):
            at = slice((j % 2) * 64 + x * 8, (j % 2) * 64 + x * 8 + 8)
            if j == 0:
                tile = jnp.where(low, zprev[at, :] * zm, znext[at, :] * zp)
            elif j == 1:
                tile = jnp.where(low, zprev[at, :], znext[at, :])
            else:
                tile = ends[at, :]
            slabs[j * 64 + x * 8 : j * 64 + x * 8 + 8, :] = tile
            start, count = REACH[j]
            for xout, first in ((xlow, 0), (xhigh, 8 - count)):
                if first <= x < first + count:
                    xout[start + (x - first) * 8 : start + (x - first) * 8 + 8, :] = tile


EDGES4 = ((-1, 3, 0), (8, 3, 3), (-2, 2, 6), (9, 2, 8), (-3, 1, 10), (10, 1, 11))
EDGES3 = ((-1, 2, 0), (8, 2, 2), (-2, 1, 4), (9, 1, 5))
EDGES2 = ((-1, 1, 0), (8, 1, 1))
COEF_AT = RHS * 12
ENDS_AT = ((COEF_AT + 24, EDGES3), (COEF_AT + 30, EDGES2), (COEF_AT + 32, EDGES2), (COEF_AT + 34, ()))
FACE_AT = (COEF_AT + 34, COEF_AT + 58, COEF_AT + 74, COEF_AT + 90)
EDGE_ROWS = 384


def pack_edges(slabs, xprev, xnext, sprev, snext, ylow, yhigh, kept):
    def put(table, to, prev, nxt, before, after):
        for x, rows, at in table:
            tile = prev[pl.ds(before + x * 8, 8), :] if x < 0 else nxt[pl.ds(after + (x - 8) * 8, 8), :]
            ylow[pl.ds(to + at, rows), :] = tile[:rows]
            yhigh[pl.ds(to + at, rows), :] = tile[8 - rows :]

    for r in range(RHS):
        put(EDGES4, r * 12, xprev, xnext, r * 32 + 32, r * 32)
    for i in range(4):
        start = face_at(RHS + i, 0)[0]
        put(EDGES3, COEF_AT + i * 6, xprev, xnext, start + 24, start)
        start, count = REACH[i]
        put(ENDS_AT[i][1], ENDS_AT[i][0], sprev, snext, start + count * 8, start)
        for x in range(8):
            tile = slabs[i * 64 + x * 8 : i * 64 + x * 8 + 8, :]
            at = FACE_AT[i] + x * count
            ylow[at : at + count, :] = tile[:count]
            yhigh[at : at + count, :] = tile[8 - count :]
    keep_faces(xprev, xnext, kept)


def keep_faces(prev, nxt, kept):
    kept[:FACE_ROWS, :] = prev[:, :]
    kept[FACE_ROWS:, :] = nxt[:, :]


WIDE = 512
NARROW = 256


def steps_gram(
    flags, fields, slabs, kept, sprev, snext, held, eprev, enext,
    basis, packed, ea, eb, es, ec, main, side, turn,
):
    lane = lanes()
    lane8 = lane % 8
    row = lax.broadcasted_iota(jnp.int32, (8, 128), 0)
    xm, xp, ym, yp, zm, zp = [flags[i] for i in range(6)]

    def fill(dst, base, wide_field, own, xs, count, ys, ycount, table, edge_at):
        size = 32 if wide_field else 16
        own_at, halo_at = ((8, 24), (16, 0)) if wide_field else ((0,), (8,))
        todo = []
        for x in range(8):
            todo.append((own_at, x + 4, 0, own[0][pl.ds(own[1] + x * 8, 8), :]))
            todo.append((halo_at, x + 4, 8 - ycount, ys[0][0][pl.ds(ys[0][1] + x * ycount, ycount), :] * ym))
            todo.append((halo_at, x + 4, 0, ys[1][0][pl.ds(ys[1][1] + x * ycount, ycount), :] * yp))
        for i in range(count):
            (low, low_at), (high, high_at) = xs
            todo.append((own_at, 4 - count + i, 0, low[pl.ds(low_at + i * 8, 8), :] * xm))
            todo.append((own_at, 12 + i, 0, high[pl.ds(high_at + i * 8, 8), :] * xp))
        for x, rows, at in table:
            m = xm if x < 0 else xp
            todo.append((halo_at, x + 4, 8 - rows, eprev[pl.ds(edge_at + at, rows), :] * (m * ym)))
            todo.append((halo_at, x + 4, 0, enext[pl.ds(edge_at + at, rows), :] * (m * yp)))
        for offsets, x, at, value in todo:
            for offset in offsets:
                dst[pl.ds(base + x * size + offset + at, value.shape[0]), :] = value

    def faces(start):
        return (held, start), (held, FACE_ROWS + start)

    def fill_rhs(i, carry):
        for u in range(FILLS):
            r = i * FILLS + u
            xs = (kept, r * 32), (kept, FACE_ROWS + r * 32)
            fill(ea, r * WIDE, True, (fields, r * 64), xs, 4, faces(r * 32), 4, EDGES4, r * 12)
        values = [fields[pl.ds((i * FILLS + u) * 64 + x * 8, 8), :] for u in range(FILLS) for x in range(8)]
        for u in range(FILLS):
            for x in range(8):
                basis[pl.ds(x * 8 * COLS + i * FILLS + u, 8, stride=COLS), :] = values[u * 8 + x]
        return carry

    lax.fori_loop(0, RHS // FILLS, fill_rhs, 0)
    for i in range(4):
        start = face_at(RHS + i, 0)[0]
        own, xs = (fields, (RHS + i) * 64), ((kept, start), (kept, FACE_ROWS + start))
        fill(ec, i * NARROW, False, own, xs, 3, faces(start), 3, EDGES3, COEF_AT + i * 6)
        at, count = REACH[i]
        own, xs = (slabs, i * 64), ((sprev, at), (snext, at))
        ys = (eprev, FACE_AT[i]), (enext, FACE_AT[i])
        fill(es, i * NARROW, False, own, xs, count, ys, count, ENDS_AT[i][1], ENDS_AT[i][0])

    for x in range(16):
        for tile in range(2):
            at = x * 16 + tile * 8
            outer, inner = es[at : at + 8, :], es[2 * NARROW + at : 2 * NARROW + at + 8, :]
            pair = (jnp.where(lane8 < 4, outer, inner), jnp.where(lane8 < 4, inner, outer))
            for base, value in zip((LOW, HIGH), pair):
                for offset in ((8, 24), (16, 0))[tile]:
                    ea[base + x * 32 + offset : base + x * 32 + offset + 8, :] = value

    def weights(a, vs, ok):
        sixth = ok * F32(1 / 6)
        out = [(a - 1.0) * sixth]
        for v in vs:
            out += [(0.5 * v - 1.0) * sixth, (-0.5 * v - 1.0) * sixth]
        return out

    def make(i, carry):
        done = []
        for u in range(MAKES):
            x = 1 + i * MAKES + u
            okx = jnp.where(x < 4, xm, jnp.where(x >= 12, xp, F32(1)))
            for tile in range(2):
                at = x * 16 + tile * 8
                ok = okx * (jnp.where(row < 4, yp, ym) if tile else jnp.ones((8, 128), F32))
                cs = [ec[pl.ds(i * NARROW + at, 8), :] for i in range(4)]
                done.append((main, at, weights(cs[0], cs[1:], ok)))
                outer, inner = es[pl.ds(NARROW + at, 8), :], es[pl.ds(3 * NARROW + at, 8), :]
                for k, (pick, okz) in enumerate(((lane8 < 4, zm), (lane8 >= 4, zp))):
                    narrow = jnp.where(pick, outer, inner)
                    cs = [jnp.take_along_axis(narrow, lane8 + 8 * i, axis=1) for i in range(4)]
                    values = weights(cs[0], cs[1:], ok * jnp.where(pick, okz, F32(1)))
                    done.append((side, k * 7 * NARROW + at, values))
        for dst, at, values in done:
            for i in range(7):
                dst[pl.ds(i * NARROW + at, 8), :] = values[i]
        return carry

    lax.fori_loop(0, 14 // MAKES, make, 0)

    for s in range(1, STEPS + 1):
        src, dst = (ea, eb) if s % 2 else (eb, ea)
        last = s == STEPS

        tiles = [(x, 0) for x in range(s, 16 - s)]
        if not last:
            tiles += [(x, 1) for x in range(s + 1, 15 - s)]
        for x, tile in tiles:
            at = x * 32 + 8 + tile * 8
            both = jnp.where(lane8 == 4, src[HIGH + at : HIGH + at + 8, :], src[LOW + at : LOW + at + 8, :])
            for r in range(RHS):
                to = r * NARROW + x * 16 + tile * 8
                turn[to : to + 8, :] = rolled(both, -(8 * r + 4))

        def step(x, tile, keep, s=s, src=src, dst=dst, last=last):
            at = x * 32 + 8 + tile * 8
            small = x * 16 + tile * 8

            def apply(c, base, v, zplus, zminus):
                out = c[0] * v
                out = out + c[1] * src[pl.ds(base + at + 32, 8), :]
                out = out + c[2] * src[pl.ds(base + at - 32, 8), :]
                out = out + c[3] * src[pl.ds(base + at + 1, 8), :]
                out = out + c[4] * src[pl.ds(base + at - 1, 8), :]
                out = out + c[5] * zplus
                return out + c[6] * zminus

            def put(base, out):
                for offset in ((8, 24), (16, 0))[tile]:
                    dst[pl.ds(base + x * 32 + offset, 8), :] = out

            cs = [main[pl.ds(i * NARROW + small, 8), :] for i in range(7)]
            for r in range(RHS):
                v = src[pl.ds(r * WIDE + at, 8), :]
                over = turn[pl.ds(r * NARROW + small, 8), :]
                zplus = rolled(jnp.where(lane == 0, over, v), -1)
                zminus = rolled(jnp.where(lane == 127, over, v), 1)
                out = apply(cs, r * WIDE, v, zplus, zminus)
                if keep:
                    basis[pl.ds((x - 4) * 8 * COLS + s * RHS + r, 8, stride=COLS), :] = out
                if not last:
                    put(r * WIDE, out)
            if not last:
                for k, base in enumerate((LOW, HIGH)):
                    cs = [side[pl.ds((k * 7 + i) * NARROW + small, 8), :] for i in range(7)]
                    v = src[pl.ds(base + at, 8), :]
                    put(base, apply(cs, base, v, rolled(v, -1), rolled(v, 1)))

        def inside(i, carry, step=step):
            for u in range(OWN):
                step(4 + i * OWN + u, 0, True)
            return carry

        def outside(i, carry, s=s, step=step):
            for u in range(4 - s):
                step(s + i * (12 - s) + u, 0, False)
            return carry

        def halo(i, carry, s=s, step=step):
            for u in range(7 - s):
                step(s + 1 + i * (7 - s) + u, 1, False)
            return carry

        lax.fori_loop(0, 8 // OWN, inside, 0)
        if not last:
            lax.fori_loop(0, 2, outside, 0)
            lax.fori_loop(0, 2, halo, 0)

    zeros = jnp.zeros((128 - COLS, 256), BF16)

    def product(i, acc):
        for u in range(GRAMS):
            base = pl.multiple_of((i * GRAMS + u) * 2 * COLS, 2 * COLS)
            value = jnp.concatenate([basis[pl.ds(base, COLS), :], basis[pl.ds(base + COLS, COLS), :]], axis=1)
            high = value.astype(BF16)
            low = (value - high.astype(F32)).astype(BF16)
            acc = acc + lax.dot_general(
                wide([high, low]),
                wide([high, zeros, low, zeros]),
                (((1,), (1,)), ((), ())),
                preferred_element_type=F32,
            )
        return acc

    acc = lax.fori_loop(0, 32 // GRAMS, product, jnp.zeros((2 * COLS, 256), F32))
    gram = (acc[:COLS, :128] + acc[COLS:, 128:]) + (acc[:COLS, 128:] + acc[COLS:, :128])
    part = [gram[i * RHS : (i + 1) * RHS] for i in range(STEPS + 1)]
    lane = lax.broadcasted_iota(jnp.int32, (RHS, 128), 1)
    packed[:RHS, :] = jnp.where(
        lane < 80, part[0], jnp.where(lane < 112, rolled(part[3], 32), rolled(part[4], 48))
    )
    packed[RHS:, :] = jnp.where(
        lane < 64, rolled(part[1], -16), jnp.where(lane < 112, rolled(part[2], 32), 0.0)
    )


def solved(p, right):
    (a, b), (c, d) = p[0][:2], p[1][:2]
    scale = 1.0 / (a * d - b * c)
    inverse = ((d * scale, -(b * scale)), (-(c * scale), a * scale))
    return [[i[0] * u + i[1] * v for u, v in zip(*right)] for i in inverse]


def solve_combine(parts, basis, solution_field, residual, held, sems):
    total = parts[0]
    for i in range(1, parts.shape[0]):
        total = total + parts[i]
    first, second = total[:RHS], total[RHS:]
    lane = lax.broadcasted_iota(jnp.int32, (RHS, 128), 1)

    def span(value, start):
        return jnp.where((lane >= start) & (lane < COLS), value, 0.0)

    upper = [
        span(first, 0),
        span(rolled(second, 16), 16),
        span(rolled(second, -32), 32),
        span(rolled(first, -32), 48),
        span(rolled(first, -48), 64),
    ]
    flipped = jnp.transpose(wide(upper + [jnp.zeros((128 - COLS, 128), F32)]))
    gram = wide(
        [
            jnp.where(lane < i * RHS, flipped[i * RHS : (i + 1) * RHS], upper[i])
            for i in range(STEPS + 1)
        ]
    )
    half = 7.0 * gram + 6.0 * rolled(gram, -RHS)
    half = jnp.where(lax.broadcasted_iota(jnp.int32, (COLS, 128), 1) < KEEP, half, 0.0)
    normal = 7.0 * half[:KEEP] + 6.0 * half[RHS:]
    m = [normal[i * 8 : i * 8 + 8] for i in range(8)] + [half[:8], half[8:RHS]]
    lane = lanes()

    def column(i, c):
        return jnp.broadcast_to(m[i][:, c : c + 1], (8, 128))

    def row(value, r):
        return jnp.broadcast_to(value[r : r + 1, :], (8, 128))

    def square(r, c):
        columns = [column(r // 8, c + j) for j in range(BLOCK)]
        return [[row(columns[j], r % 8 + i) for j in range(BLOCK)] for i in range(BLOCK)]

    pivots = square(0, 0)
    for k in range(0, KEEP, BLOCK):
        i0, s = divmod(k, 8)
        inside = (lane >= k) & (lane < k + BLOCK)
        keep = list(range(i0 + 1 if s + BLOCK == 8 else i0, 10))
        columns = {i: [column(i, k + c) for c in range(BLOCK)] for i in keep}
        rows = [
            jnp.where(lane == k + d, -1.0, jnp.where(inside, 0.0, row(m[i0], s + d))) for d in range(BLOCK)
        ]
        more = k + BLOCK < KEEP
        if more:
            across, after = square(k, k + BLOCK), square(k + BLOCK, k + BLOCK)
            rights = [across[d] + [rows[d]] for d in range(BLOCK)]
        else:
            rights = [[rows[d]] for d in range(BLOCK)]
        upper = solved(pivots[:2], [pivots[d][2:] + rights[d] for d in (0, 1)])
        rest = [
            [u - (pivots[e][0] * v + pivots[e][1] * w) for u, v, w in zip(pivots[e][2:] + rights[e], *upper)]
            for e in (2, 3)
        ]
        lower = solved(rest, [r[2:] for r in rest])
        upper = [
            [u - (upper[d][0] * v + upper[d][1] * w) for u, v, w in zip(upper[d][2:], *lower)] for d in (0, 1)
        ]
        result = upper + lower
        if more:
            pivots = [
                [
                    after[d][c] - (
                        (across[0][d] * result[0][c] + across[1][d] * result[1][c])
                        + (across[2][d] * result[2][c] + across[3][d] * result[3][c])
                    )
                    for c in range(BLOCK)
                ]
                for d in range(BLOCK)
            ]
        for i in keep:
            value = jnp.where(inside, 0.0, m[i])
            for c in range(BLOCK):
                value = value - columns[i][c] * result[c][-1]
            m[i] = value
    coef = wide(m[8:])
    mixed = 7.0 * coef + 6.0 * rolled(coef, RHS)
    both = wide([coef, mixed])
    high = both.astype(BF16).astype(F32)
    mid = (both - high).astype(BF16).astype(F32)
    low = both - high - mid
    lane = lax.broadcasted_iota(jnp.int32, (2 * RHS, 128), 1)

    def tripled(value, parts):
        left = value if parts == 1 else jnp.where(lane < 80, value, rolled(value, 80))
        right = jnp.where(lane < 32, rolled(value, -48), 0.0) if parts > 1 else jnp.zeros_like(value)
        if parts == 3:
            right = jnp.where((lane >= 32) & (lane < 112), rolled(value, 32), right)
        return jnp.concatenate([left, right], axis=1)

    factors = wide([tripled(high, 3), tripled(mid, 2), tripled(low, 1)[RHS:]]).astype(BF16)
    zeros = jnp.zeros((16, 256), BF16)

    def combine(i, carry):
        done = []
        for u in range(PAIRS):
            base = pl.multiple_of((i * PAIRS + u) * 2 * COLS, 2 * COLS)
            value = jnp.concatenate([basis[pl.ds(base, COLS), :], basis[pl.ds(base + COLS, COLS), :]], axis=1)
            high = value.astype(BF16)
            rest = value - high.astype(F32)
            mid = rest.astype(BF16)
            low = (rest - mid.astype(F32)).astype(BF16)
            out = jnp.dot(factors, wide([high, mid, low, zeros]), preferred_element_type=F32)
            mixed = out[RHS : 2 * RHS] + (out[3 * RHS : 4 * RHS] + out[4 * RHS :])
            done.append((out[:RHS] + out[2 * RHS : 3 * RHS], value[:RHS] - mixed))
        for u in range(PAIRS):
            for c in range(2):
                at = 2 * (i * PAIRS + u) + c
                held[pl.ds(at, RHS, stride=64), :] = done[u][0][:, c * 128 : (c + 1) * 128]
                held[pl.ds(1024 + at, RHS, stride=64), :] = done[u][1][:, c * 128 : (c + 1) * 128]
        return carry

    count = 32 // PAIRS
    copies = []
    for i in range(count):
        combine(i, 0)
        rows = pl.ds(i * 2 * PAIRS, 2 * PAIRS)
        for k, out in enumerate((solution_field, residual)):
            src = held.reshape(2, RHS, 64, 128).at[k, :, rows, :]
            copies.append(pltpu.make_async_copy(src, out.at[:, rows, :], sems.at[i * 2 + k]))
            copies[-1].start()
    for copy in copies:
        copy.wait()


def call(kernel, ins, outs, scratch=(), smem=False, hbm=False):
    vmem = pl.BlockSpec(memory_space=pltpu.VMEM)
    specs = [vmem] * len(ins)
    if smem:
        specs[0] = pl.BlockSpec(memory_space=pltpu.SMEM)
    return pl.pallas_call(
        kernel,
        out_shape=[jax.ShapeDtypeStruct(s, F32) for s in outs],
        in_specs=specs,
        out_specs=[pl.BlockSpec(memory_space=pl.ANY) if hbm else vmem] * len(outs),
        scratch_shapes=[pltpu.VMEM(s, F32) if isinstance(s, tuple) else s for s in scratch],
        compiler_params=pltpu.CompilerParams(vmem_limit_bytes=LIMIT),
    )(*ins)


def shift(value, axis, by):
    count = lax.axis_size(axis)
    return lax.ppermute(value, axis, [(i, (i + by) % count) for i in range(count)])


def gathered(value, axis):
    count = lax.axis_size(axis)
    return lax.all_to_all(jnp.broadcast_to(value[None], (count,) + value.shape), axis, 0, 0)


def shards(right_side, absorption, velocity):
    axes = ("gx", "gy", ("zx", "core"))
    ends = []
    for axis in axes:
        at = lax.axis_index(axis)
        ends += [at > 0, at < lax.axis_size(axis) - 1]
    flags = jnp.stack(ends).astype(F32)
    fields = jnp.concatenate([right_side, absorption[None], velocity], axis=0).reshape((RHS + 4) * 64, 128)
    face = (FACE_ROWS, 128)
    ends_z, xlow, xhigh, ylow, yhigh = call(pack_own, [fields], [(128, 128), face, face, face, face])
    xprev = shift(xhigh, "gx", 1)
    xnext = shift(xlow, "gx", -1)
    zprev = shift(ends_z, axes[2], 1)
    znext = shift(ends_z, axes[2], -1)
    slabs, slow, shigh = call(
        pack_ends, [flags, ends_z, zprev, znext], [(256, 128), (128, 128), (128, 128)], smem=True
    )
    sprev = shift(shigh, "gx", 1)
    snext = shift(slow, "gx", -1)
    yprev = shift(yhigh, "gy", 1)
    ynext = shift(ylow, "gy", -1)
    edge = (EDGE_ROWS, 128)
    elow, ehigh, kept = call(pack_edges, [slabs, xprev, xnext, sprev, snext], [edge, edge, (2 * FACE_ROWS, 128)])
    eprev = shift(ehigh, "gy", 1)
    enext = shift(elow, "gy", -1)
    (held,) = call(keep_faces, [yprev, ynext], [(2 * FACE_ROWS, 128)])
    basis, packed = call(
        steps_gram,
        [flags, fields, slabs, kept, sprev, snext, held, eprev, enext],
        [(64 * COLS, 128), (2 * RHS, 128)],
        [(18 * WIDE, 128)] * 2 + [(n * NARROW, 128) for n in (4, 4, 7, 14, RHS)],
        smem=True,
    )
    packed = packed + shift(packed, "core", 1)
    packed = gathered(packed, ("gx", "zx")).sum(0)
    parts = gathered(packed, "gy")
    solution_field, residual = call(
        solve_combine,
        [parts, basis],
        [(RHS, 64, 128), (RHS, 64, 128)],
        [pltpu.VMEM((2048, 128), F32), pltpu.SemaphoreType.DMA((64 // PAIRS,))],
        hbm=True,
    )
    return solution_field.reshape(right_side.shape), residual.reshape(right_side.shape)


def solution(mesh):
    nx, ny, nz = mesh.devices.shape
    split = Mesh(mesh.devices.reshape(nx, ny, nz // 2, 2), ("gx", "gy", "zx", "core"))
    z = ("zx", "core")
    return jax.shard_map(
        shards,
        mesh=split,
        in_specs=(P(None, "gx", "gy", z), P("gx", "gy", z), P(None, "gx", "gy", z)),
        out_specs=(P(None, "gx", "gy", z), P(None, "gx", "gy", z)),
        check_vma=False,
    )
```

profile of v0, /device:TPU:2, one launch (start us, length us, event | category | flops | bytes accessed | tf_op | source)
XLA Modules:
  0.0 74.5 jit_solution(9575165831978385117)
XLA Ops:
  0.6 1.2 %pad_maximum_fusion = f32[20,8,8,128]{3,2,1,0:T(8,128)S(1)} fusion(f32[3,8,8,128]{3,2,1,0:T(8,128)} %param.5, f32[1,8,8,128]{3,2,1,0:T(8,128)} %bitcast.12, f32[16,8,8,128]{3,2,1,0:T(8,128)} %param.3), kind=kLoop, calls=%fused_computation | loop fusion | flops 327680 | bytes 1310720 | tf_op jit(solution)/shard_map/concatenate | solution.py:484
  1.8 0.3 shard_map.50
  2.1 1.7 %collective-permute-start.2 = (f32[608,128]{1,0:T(8,128)S(1)}, f32[608,128]{1,0:T(8,128)S(1)}, u32[]{:S(2)}, u32[]{:S(2)}) collective-permute-start(f32[608,128]{1,0:T(8,128)S(1)} %get-tuple-element.19), channel_id=1, source_target_pairs={{0,64},{64,128},{128,192},{192,0},{1,65},{65,129},{129,193},{193,1... | collective-permute-start | bytes 933896 | tf_op jit(solution)/shard_map/ppermute | solution.py:469
  3.8 1.7 %collective-permute-start.3 = (f32[608,128]{1,0:T(8,128)S(1)}, f32[608,128]{1,0:T(8,128)S(1)}, u32[]{:S(2)}, u32[]{:S(2)}) collective-permute-start(f32[608,128]{1,0:T(8,128)S(1)} %get-tuple-element.20), channel_id=1, source_target_pairs={{0,192},{64,0},{128,64},{192,128},{1,193},{65,1},{129,65},{193,129... | collective-permute-start | bytes 933896 | tf_op jit(solution)/shard_map/ppermute | solution.py:469
  5.4 0.0 collective-permute-start.1
  5.4 0.5 collective-permute-start
  5.9 0.1 stack.27
  6.1 1.3 %collective-permute-done.1.znext = f32[128,128]{1,0:T(8,128)S(1)} collective-permute-done((f32[128,128]{1,0:T(8,128)S(1)}, f32[128,128]{1,0:T(8,128)S(1)}, u32[]{:S(2)}, u32[]{:S(2)}) %collective-permute-start.1) | collective-permute-done | bytes 65568 | tf_op jit(solution)/shard_map/ppermute | solution.py:469
  7.3 2.4 %collective-permute-done.zprev = f32[128,128]{1,0:T(8,128)S(1)} collective-permute-done((f32[128,128]{1,0:T(8,128)S(1)}, f32[128,128]{1,0:T(8,128)S(1)}, u32[]{:S(2)}, u32[]{:S(2)}) %collective-permute-start) | collective-permute-done | bytes 65568 | tf_op jit(solution)/shard_map/ppermute | solution.py:469
  9.8 0.6 shard_map.51
  10.3 0.1 collective-permute-start.4
  10.4 1.6 %collective-permute-start.6 = (f32[608,128]{1,0:T(8,128)S(1)}, f32[608,128]{1,0:T(8,128)S(1)}, u32[]{:S(2)}, u32[]{:S(2)}) collective-permute-start(f32[608,128]{1,0:T(8,128)S(1)} %get-tuple-element.24), channel_id=1, source_target_pairs={{0,8},{8,16},{16,24},{24,32},{32,40},{40,48},{48,56},{56,0},{1,9},... | collective-permute-start | bytes 933896 | tf_op jit(solution)/shard_map/ppermute | solution.py:469
  12.1 3.9 %collective-permute-start.7 = (f32[608,128]{1,0:T(8,128)S(1)}, f32[608,128]{1,0:T(8,128)S(1)}, u32[]{:S(2)}, u32[]{:S(2)}) collective-permute-start(f32[608,128]{1,0:T(8,128)S(1)} %get-tuple-element.25), channel_id=1, source_target_pairs={{0,56},{8,0},{16,8},{24,16},{32,24},{40,32},{48,40},{56,48},{1,57}... | collective-permute-start | bytes 933896 | tf_op jit(solution)/shard_map/ppermute | solution.py:469
  16.0 0.0 collective-permute-done.4.sprev
  16.0 2.9 %collective-permute-start.5 = (f32[128,128]{1,0:T(8,128)S(1)}, f32[128,128]{1,0:T(8,128)S(1)}, u32[]{:S(2)}, u32[]{:S(2)}) collective-permute-start(f32[128,128]{1,0:T(8,128)S(1)} %get-tuple-element.22), channel_id=1, source_target_pairs={{0,192},{64,0},{128,64},{192,128},{1,193},{65,1},{129,65},{193,129... | collective-permute-start | bytes 196616 | tf_op jit(solution)/shard_map/ppermute | solution.py:469
  18.9 1.9 %collective-permute-done.5.snext = f32[128,128]{1,0:T(8,128)S(1)} collective-permute-done((f32[128,128]{1,0:T(8,128)S(1)}, f32[128,128]{1,0:T(8,128)S(1)}, u32[]{:S(2)}, u32[]{:S(2)}) %collective-permute-start.5) | collective-permute-done | bytes 65568 | tf_op jit(solution)/shard_map/ppermute | solution.py:469
  20.8 0.0 collective-permute-done.2.xprev
  20.8 0.0 collective-permute-done.3.xnext
  20.8 0.1 shard_map.52
  20.9 0.7 collective-permute-start.8
  21.6 4.0 %collective-permute-start.9 = (f32[384,128]{1,0:T(8,128)S(1)}, f32[384,128]{1,0:T(8,128)S(1)}, u32[]{:S(2)}, u32[]{:S(2)}) collective-permute-start(f32[384,128]{1,0:T(8,128)S(1)} %get-tuple-element.27), channel_id=1, source_target_pairs={{0,56},{8,0},{16,8},{24,16},{32,24},{40,32},{48,40},{56,48},{1,57}... | collective-permute-start | bytes 589832 | tf_op jit(solution)/shard_map/ppermute | solution.py:469
  25.7 0.0 collective-permute-done.6.prev
  25.7 0.0 collective-permute-done.7.nxt
  25.7 3.5 %collective-permute-done.8.eprev = f32[384,128]{1,0:T(8,128)S(1)} collective-permute-done((f32[384,128]{1,0:T(8,128)S(1)}, f32[384,128]{1,0:T(8,128)S(1)}, u32[]{:S(2)}, u32[]{:S(2)}) %collective-permute-start.8) | collective-permute-done | bytes 196640 | tf_op jit(solution)/shard_map/ppermute | solution.py:469
  29.2 0.0 collective-permute-done.9.enext
  29.2 9.4 %shard_map.54 = (f32[5120,128]{1,0:T(8,128)S(1)}, f32[32,128]{1,0:T(8,128)S(1)}) custom-call(f32[6]{0:T(128)S(1)} %convert_element_type.3.flags, f32[1280,128]{1,0:T(8,128)S(1)} %bitcast.11, f32[256,128]{1,0:T(8,128)S(1)} %get-tuple-element.18.slabs, f32[1216,128]{1,0:T(8,128)S(1)} %get-tuple-element.23.kept, f32[128,128]{1,0:T(8,128)S(1)} %collective-permute-done.4.sprev, ...), custom_call_target="tpu_custom_call" | custom-call | tf_op jit(solution)/shard_map/pallas_call | solution.py:457
  38.6 0.2 collective-permute-start.10
  38.8 1.2 %collective-permute-done.10 = f32[32,128]{1,0:T(8,128)S(1)} collective-permute-done((f32[32,128]{1,0:T(8,128)S(1)}, f32[32,128]{1,0:T(8,128)S(1)}, u32[]{:S(2)}, u32[]{:S(2)}) %collective-permute-start.10) | collective-permute-done | bytes 16416 | tf_op jit(solution)/shard_map/ppermute | solution.py:469
  40.0 14.5 %all_to_all.10 = f32[16,32,128]{2,1,0:T(8,128)S(1)} all-to-all(f32[16,32,128]{2,1,0:T(8,128)S(1)} %broadcast_in_dim.7), channel_id=1, replica_groups=mesh['gx'=4,'gy'=8,'zx'=4,'core'=2] {'gx','zx'}, dimensions={0} | all-to-all | bytes 524288 | tf_op jit(solution)/shard_map/all_to_all | solution.py:474
  54.5 15.3 %all_to_all.11.parts = f32[8,32,128]{2,1,0:T(8,128)S(1)} all-to-all(f32[8,32,128]{2,1,0:T(8,128)S(1)} %broadcast_in_dim.8), channel_id=1, replica_groups=mesh['gx'=4,'gy'=8,'zx'=4,'core'=2] {'gy'}, dimensions={0} | all-to-all | bytes 262144 | tf_op jit(solution)/shard_map/all_to_all | solution.py:474
  69.8 4.5 %shard_map.55 = (f32[16,64,128]{2,1,0:T(8,128)}, f32[16,64,128]{2,1,0:T(8,128)}) custom-call(f32[8,32,128]{2,1,0:T(8,128)S(1)} %all_to_all.11.parts, f32[5120,128]{1,0:T(8,128)S(1)} %get-tuple-element.29.basis), custom_call_target="tpu_custom_call" | custom-call | tf_op jit(solution)/shard_map/pallas_call | solution.py:457
  (6 shorter events, 0.1 us)
Async XLA Ops:
  2.1 18.7 %collective-permute-start.2 = (f32[608,128]{1,0:T(8,128)S(1)}, f32[608,128]{1,0:T(8,128)S(1)}, u32[]{:S(2)}, u32[]{:S(2)}) collective-permute-start(f32[608,128]{1,0:T(8,128)S(1)} %get-tuple-element.19), channel_id=1, source_target_pairs={{0,64},{64,128},{128,192},{192,0},{1,65},{65,129},{129,193},{193,1... | collective-permute-start | bytes 933896 | tf_op jit(solution)/shard_map/ppermute | solution.py:469
  3.8 17.0 %collective-permute-start.3 = (f32[608,128]{1,0:T(8,128)S(1)}, f32[608,128]{1,0:T(8,128)S(1)}, u32[]{:S(2)}, u32[]{:S(2)}) collective-permute-start(f32[608,128]{1,0:T(8,128)S(1)} %get-tuple-element.20), channel_id=1, source_target_pairs={{0,192},{64,0},{128,64},{192,128},{1,193},{65,1},{129,65},{193,129... | collective-permute-start | bytes 933896 | tf_op jit(solution)/shard_map/ppermute | solution.py:469
  5.4 1.9 %collective-permute-start.1 = (f32[128,128]{1,0:T(8,128)S(1)}, f32[128,128]{1,0:T(8,128)S(1)}, u32[]{:S(2)}, u32[]{:S(2)}) collective-permute-start(f32[128,128]{1,0:T(8,128)S(1)} %get-tuple-element.17.ends), channel_id=1, source_target_pairs={{0,7},{1,0},{2,1},{3,2},{4,3},{5,4},{6,5},{7,6},{8,15},{9,8},{10,9... | collective-permute-start | bytes 196616 | tf_op jit(solution)/shard_map/ppermute | solution.py:469
  5.4 4.3 %collective-permute-start = (f32[128,128]{1,0:T(8,128)S(1)}, f32[128,128]{1,0:T(8,128)S(1)}, u32[]{:S(2)}, u32[]{:S(2)}) collective-permute-start(f32[128,128]{1,0:T(8,128)S(1)} %get-tuple-element.17.ends), channel_id=1, source_target_pairs={{0,1},{1,2},{2,3},{3,4},{4,5},{5,6},{6,7},{7,0},{8,9},{9,10},{10,1... | collective-permute-start | bytes 196616 | tf_op jit(solution)/shard_map/ppermute | solution.py:469
  10.3 5.7 %collective-permute-start.4 = (f32[128,128]{1,0:T(8,128)S(1)}, f32[128,128]{1,0:T(8,128)S(1)}, u32[]{:S(2)}, u32[]{:S(2)}) collective-permute-start(f32[128,128]{1,0:T(8,128)S(1)} %get-tuple-element.21), channel_id=1, source_target_pairs={{0,64},{64,128},{128,192},{192,0},{1,65},{65,129},{129,193},{193,1... | collective-permute-start | bytes 196616 | tf_op jit(solution)/shard_map/ppermute | solution.py:469
  10.4 15.3 %collective-permute-start.6 = (f32[608,128]{1,0:T(8,128)S(1)}, f32[608,128]{1,0:T(8,128)S(1)}, u32[]{:S(2)}, u32[]{:S(2)}) collective-permute-start(f32[608,128]{1,0:T(8,128)S(1)} %get-tuple-element.24), channel_id=1, source_target_pairs={{0,8},{8,16},{16,24},{24,32},{32,40},{40,48},{48,56},{56,0},{1,9},... | collective-permute-start | bytes 933896 | tf_op jit(solution)/shard_map/ppermute | solution.py:469
  12.1 13.6 %collective-permute-start.7 = (f32[608,128]{1,0:T(8,128)S(1)}, f32[608,128]{1,0:T(8,128)S(1)}, u32[]{:S(2)}, u32[]{:S(2)}) collective-permute-start(f32[608,128]{1,0:T(8,128)S(1)} %get-tuple-element.25), channel_id=1, source_target_pairs={{0,56},{8,0},{16,8},{24,16},{32,24},{40,32},{48,40},{56,48},{1,57}... | collective-permute-start | bytes 933896 | tf_op jit(solution)/shard_map/ppermute | solution.py:469
  16.0 4.8 %collective-permute-start.5 = (f32[128,128]{1,0:T(8,128)S(1)}, f32[128,128]{1,0:T(8,128)S(1)}, u32[]{:S(2)}, u32[]{:S(2)}) collective-permute-start(f32[128,128]{1,0:T(8,128)S(1)} %get-tuple-element.22), channel_id=1, source_target_pairs={{0,192},{64,0},{128,64},{192,128},{1,193},{65,1},{129,65},{193,129... | collective-permute-start | bytes 196616 | tf_op jit(solution)/shard_map/ppermute | solution.py:469
  20.9 8.3 %collective-permute-start.8 = (f32[384,128]{1,0:T(8,128)S(1)}, f32[384,128]{1,0:T(8,128)S(1)}, u32[]{:S(2)}, u32[]{:S(2)}) collective-permute-start(f32[384,128]{1,0:T(8,128)S(1)} %get-tuple-element.26), channel_id=1, source_target_pairs={{0,8},{8,16},{16,24},{24,32},{32,40},{40,48},{48,56},{56,0},{1,9},... | collective-permute-start | bytes 589832 | tf_op jit(solution)/shard_map/ppermute | solution.py:469
  21.6 7.6 %collective-permute-start.9 = (f32[384,128]{1,0:T(8,128)S(1)}, f32[384,128]{1,0:T(8,128)S(1)}, u32[]{:S(2)}, u32[]{:S(2)}) collective-permute-start(f32[384,128]{1,0:T(8,128)S(1)} %get-tuple-element.27), channel_id=1, source_target_pairs={{0,56},{8,0},{16,8},{24,16},{32,24},{40,32},{48,40},{56,48},{1,57}... | collective-permute-start | bytes 589832 | tf_op jit(solution)/shard_map/ppermute | solution.py:469
  38.6 1.4 %collective-permute-start.10 = (f32[32,128]{1,0:T(8,128)S(1)}, f32[32,128]{1,0:T(8,128)S(1)}, u32[]{:S(2)}, u32[]{:S(2)}) collective-permute-start(f32[32,128]{1,0:T(8,128)S(1)} %get-tuple-element.28), channel_id=1, source_target_pairs={{0,1},{1,0},{2,3},{3,2},{4,5},{5,4},{6,7},{7,6},{8,9},{9,8},{10,11... | collective-permute-start | bytes 49160 | tf_op jit(solution)/shard_map/ppermute | solution.py:469
where the time goes:
time: 74.7 us; the launch traced here: 74.5 us
  blocking collectives  29.7 us (40%)
  starting transfers between devices  17.3 us (23%)
  Pallas kernels  14.9 us (20%)
  waiting for transfers between devices  10.3 us (14%)
  other arithmetic  1.19 us (2%)
  between operations  0.87 us (1%)
    all_to_all x2, blocking collectives, gathered(): lax.all_to_all(jnp.broadcast_to(value[None], (count,) + value.shape), axi...  29.7 us
    ppermute x11, starting transfers between devices, shift(): lax.ppermute(value, axis, [(i, (i + by) % count) for i in range(count)])  17.3 us
    pallas_call x6, Pallas kernels, call(): pl.pallas_call(kernel, out_shape=[jax.ShapeDtypeStruct(s, F32) for s in o...  14.9 us
    ppermute x11, waiting for transfers between devices, shift(): lax.ppermute(value, axis, [(i, (i + by) % count) for i in range(count)])  10.3 us
  transfers between devices with their start and end apart: 11, of which 5 were waited for; matrix products, arithmetic and copies ran while one was open for 0% of the time, Pallas kernels for 1%

commit v1 on v0

--- a/solution.py
+++ b/solution.py
@@ -26,6 +26,15 @@
     return lax.broadcasted_iota(jnp.int32, (8, 128), 1)
 
 
+def borders():
+    places = [(lax.axis_index(axis), lax.axis_size(axis)) for axis in ("gx", "gy")]
+    places.append((lax.axis_index("zx") * 2 + lax.axis_index("core"), lax.axis_size("zx") * 2))
+    out = []
+    for at, size in places:
+        out += [jnp.where(at > 0, F32(1), F32(0)), jnp.where(at < size - 1, F32(1), F32(0))]
+    return out
+
+
 def rolled(x, amount):
     amount = amount % x.shape[-1]
     return x if amount == 0 else pltpu.roll(x, amount, x.ndim - 1)
@@ -64,18 +73,12 @@
 REACH = ((0, 3), (24, 2), (40, 2), (56, 1))
 
 
-def pack_ends(flags, ends, zprev, znext, slabs, xlow, xhigh):
-    low = lanes() % 8 < 4
-    zm, zp = flags[4], flags[5]
+def pack_ends(ends, mate, other, slabs, xlow, xhigh):
+    from_mate = (lanes() % 8 < 4) == (lax.axis_index("core") == 1)
     for j in range(4):
         for x in range(8):
             at = slice((j % 2) * 64 + x * 8, (j % 2) * 64 + x * 8 + 8)
-            if j == 0:
-                tile = jnp.where(low, zprev[at, :] * zm, znext[at, :] * zp)
-            elif j == 1:
-                tile = jnp.where(low, zprev[at, :], znext[at, :])
-            else:
-                tile = ends[at, :]
+            tile = ends[at, :] if j > 1 else jnp.where(from_mate, mate[at, :], other[at, :])
             slabs[j * 64 + x * 8 : j * 64 + x * 8 + 8, :] = tile
             start, count = REACH[j]
             for xout, first in ((xlow, 0), (xhigh, 8 - count)):
@@ -124,13 +127,14 @@
 
 
 def steps_gram(
-    flags, fields, slabs, kept, sprev, snext, held, eprev, enext,
+    fields, slabs, kept, sprev, snext, held, eprev, enext,
     basis, packed, ea, eb, es, ec, main, side, turn,
 ):
     lane = lanes()
     lane8 = lane % 8
     row = lax.broadcasted_iota(jnp.int32, (8, 128), 0)
-    xm, xp, ym, yp, zm, zp = [flags[i] for i in range(6)]
+    xm, xp, ym, yp, zm, zp = borders()
+    beyond_ends = jnp.where(lane8 < 4, zm, zp)
 
     def fill(dst, base, wide_field, own, xs, count, ys, ycount, table, edge_at):
         size = 32 if wide_field else 16
@@ -179,7 +183,7 @@
     for x in range(16):
         for tile in range(2):
             at = x * 16 + tile * 8
-            outer, inner = es[at : at + 8, :], es[2 * NARROW + at : 2 * NARROW + at + 8, :]
+            outer, inner = es[at : at + 8, :] * beyond_ends, es[2 * NARROW + at : 2 * NARROW + at + 8, :]
             pair = (jnp.where(lane8 < 4, outer, inner), jnp.where(lane8 < 4, inner, outer))
             for base, value in zip((LOW, HIGH), pair):
                 for offset in ((8, 24), (16, 0))[tile]:
@@ -449,11 +453,9 @@
         copy.wait()
 
 
-def call(kernel, ins, outs, scratch=(), smem=False, hbm=False):
+def call(kernel, ins, outs, scratch=(), hbm=False):
     vmem = pl.BlockSpec(memory_space=pltpu.VMEM)
     specs = [vmem] * len(ins)
-    if smem:
-        specs[0] = pl.BlockSpec(memory_space=pltpu.SMEM)
     return pl.pallas_call(
         kernel,
         out_shape=[jax.ShapeDtypeStruct(s, F32) for s in outs],
@@ -475,21 +477,17 @@
 
 
 def shards(right_side, absorption, velocity):
-    axes = ("gx", "gy", ("zx", "core"))
-    ends = []
-    for axis in axes:
-        at = lax.axis_index(axis)
-        ends += [at > 0, at < lax.axis_size(axis) - 1]
-    flags = jnp.stack(ends).astype(F32)
     fields = jnp.concatenate([right_side, absorption[None], velocity], axis=0).reshape((RHS + 4) * 64, 128)
     face = (FACE_ROWS, 128)
     ends_z, xlow, xhigh, ylow, yhigh = call(pack_own, [fields], [(128, 128), face, face, face, face])
     xprev = shift(xhigh, "gx", 1)
     xnext = shift(xlow, "gx", -1)
-    zprev = shift(ends_z, axes[2], 1)
-    znext = shift(ends_z, axes[2], -1)
+    count = 2 * lax.axis_size("zx")
+    mate = lax.ppermute(ends_z, ("zx", "core"), [(i, i ^ 1) for i in range(count)])
+    pairs = [((2 * i + 1) % count, (2 * i + 2) % count) for i in range(count // 2)]
+    other = lax.ppermute(ends_z, ("zx", "core"), pairs + [(b, a) for a, b in pairs])
     slabs, slow, shigh = call(
-        pack_ends, [flags, ends_z, zprev, znext], [(256, 128), (128, 128), (128, 128)], smem=True
+        pack_ends, [ends_z, mate, other], [(256, 128), (128, 128), (128, 128)]
     )
     sprev = shift(shigh, "gx", 1)
     snext = shift(slow, "gx", -1)
@@ -502,10 +500,9 @@
     (held,) = call(keep_faces, [yprev, ynext], [(2 * FACE_ROWS, 128)])
     basis, packed = call(
         steps_gram,
-        [flags, fields, slabs, kept, sprev, snext, held, eprev, enext],
+        [fields, slabs, kept, sprev, snext, held, eprev, enext],
         [(64 * COLS, 128), (2 * RHS, 128)],
         [(18 * WIDE, 128)] * 2 + [(n * NARROW, 128) for n in (4, 4, 7, 14, RHS)],
-        smem=True,
     )
     packed = packed + shift(packed, "core", 1)
     packed = gathered(packed, ("gx", "zx")).sum(0)

time: 74.7 us -> 72.9 us (0.976)
  starting transfers between devices: 17.3 us -> 19.1 us
  waiting for transfers between devices: 10.3 us -> 8.5 us
  Pallas kernels: 14.9 us -> 13.8 us
    ppermute x11 -> x9, waiting for transfers between devices: 10.3 us -> 6.42 us  [shift(): lax.ppermute(value, axis, [(i, (i + by) % count) for i in range(count)])]
    ppermute x0 -> x2, waiting for transfers between devices: none -> 2.09 us  [the longest x1 2.08 us: shards(): lax.ppermute(ends_z, ('zx', 'core'), pairs + [(b, a) for a, b in pairs])]
    ppermute x0 -> x2, starting transfers between devices: none -> 1.61 us  [the longest x1 1.6 us: shards(): lax.ppermute(ends_z, ('zx', 'core'), [(i, i ^ 1) for i in range(count)])]
    pallas_call x6, Pallas kernels: 14.9 us -> 13.8 us  [call(): pl.pallas_call(kernel, out_shape=[jax.ShapeDtypeStruct(s, F32) for s in o...]
    ppermute x11 -> x9, starting transfers between devices: 17.3 us -> 17.5 us  [shift(): lax.ppermute(value, axis, [(i, (i + by) % count) for i in range(count)])]
  transfers between devices with their start and end apart: 11 -> 11, of which waited for: 5 -> 4; matrix products, arithmetic and copies ran while one was open for 0% -> 0% of each run, Pallas kernels for 1% -> 0%
where the time goes in v1:
time: 72.9 us; the launch traced here: 72.7 us
  blocking collectives  29.2 us (40%)
  starting transfers between devices  19.1 us (26%)
  Pallas kernels  13.8 us (19%)
  waiting for transfers between devices  8.5 us (12%)
  other arithmetic  1.19 us (2%)
  between operations  0.86 us (1%)
    all_to_all x2, blocking collectives, gathered(): lax.all_to_all(jnp.broadcast_to(value[None], (count,) + value.shape), axi...  29.2 us
    ppermute x9, starting transfers between devices, shift(): lax.ppermute(value, axis, [(i, (i + by) % count) for i in range(count)])  17.5 us
    pallas_call x6, Pallas kernels, call(): pl.pallas_call(kernel, out_shape=[jax.ShapeDtypeStruct(s, F32) for s in o...  13.8 us
    ppermute x9, waiting for transfers between devices, shift(): lax.ppermute(value, axis, [(i, (i + by) % count) for i in range(count)])  6.42 us
    ppermute x1, waiting for transfers between devices, shards(): lax.ppermute(ends_z, ('zx', 'core'), pairs + [(b, a) for a, b in pairs])  2.08 us
    ppermute x1, starting transfers between devices, shards(): lax.ppermute(ends_z, ('zx', 'core'), [(i, i ^ 1) for i in range(count)])  1.6 us
  transfers between devices with their start and end apart: 11, of which 4 were waited for; matrix products, arithmetic and copies ran while one was open for 0% of the time, Pallas kernels for 0%

profile of v1, /device:TPU:2, one launch (start us, length us, event | category | flops | bytes accessed | tf_op | source)
XLA Modules:
  0.0 72.7 jit_solution(5681901725359751881)
XLA Ops:
  0.6 1.2 %pad_maximum_fusion = f32[20,8,8,128]{3,2,1,0:T(8,128)S(1)} fusion(f32[3,8,8,128]{3,2,1,0:T(8,128)} %param.5, f32[1,8,8,128]{3,2,1,0:T(8,128)} %bitcast.6, f32[16,8,8,128]{3,2,1,0:T(8,128)} %param.3), kind=kLoop, calls=%fused_computation | loop fusion | flops 327680 | bytes 1310720 | tf_op jit(solution)/shard_map/concatenate | solution.py:480
  1.8 0.3 shard_map.50
  2.1 1.7 %collective-permute-start.2 = (f32[608,128]{1,0:T(8,128)S(1)}, f32[608,128]{1,0:T(8,128)S(1)}, u32[]{:S(2)}, u32[]{:S(2)}) collective-permute-start(f32[608,128]{1,0:T(8,128)S(1)} %get-tuple-element.19), channel_id=1, source_target_pairs={{0,64},{64,128},{128,192},{192,0},{1,65},{65,129},{129,193},{193,1... | collective-permute-start | bytes 933896 | tf_op jit(solution)/shard_map/ppermute | solution.py:471
  3.8 1.7 %collective-permute-start.3 = (f32[608,128]{1,0:T(8,128)S(1)}, f32[608,128]{1,0:T(8,128)S(1)}, u32[]{:S(2)}, u32[]{:S(2)}) collective-permute-start(f32[608,128]{1,0:T(8,128)S(1)} %get-tuple-element.20), channel_id=1, source_target_pairs={{0,192},{64,0},{128,64},{192,128},{1,193},{65,1},{129,65},{193,129... | collective-permute-start | bytes 933896 | tf_op jit(solution)/shard_map/ppermute | solution.py:471
  5.4 0.0 collective-permute-start.1
  5.4 1.6 %collective-permute-start = (f32[128,128]{1,0:T(8,128)S(1)}, f32[128,128]{1,0:T(8,128)S(1)}, u32[]{:S(2)}, u32[]{:S(2)}) collective-permute-start(f32[128,128]{1,0:T(8,128)S(1)} %get-tuple-element.17.ends), channel_id=1, source_target_pairs={{0,1},{1,0},{2,3},{3,2},{4,5},{5,4},{6,7},{7,6},{8,9},{9,8},{10,11... | collective-permute-start | bytes 196616 | tf_op jit(solution)/shard_map/ppermute | solution.py:486
  7.0 2.1 %collective-permute-done.1.other = f32[128,128]{1,0:T(8,128)S(1)} collective-permute-done((f32[128,128]{1,0:T(8,128)S(1)}, f32[128,128]{1,0:T(8,128)S(1)}, u32[]{:S(2)}, u32[]{:S(2)}) %collective-permute-start.1) | collective-permute-done | bytes 65568 | tf_op jit(solution)/shard_map/ppermute | solution.py:488
  9.1 0.0 collective-permute-done.mate
  9.1 0.4 collective-permute-start.4
  9.6 1.9 %collective-permute-start.6 = (f32[608,128]{1,0:T(8,128)S(1)}, f32[608,128]{1,0:T(8,128)S(1)}, u32[]{:S(2)}, u32[]{:S(2)}) collective-permute-start(f32[608,128]{1,0:T(8,128)S(1)} %get-tuple-element.24), channel_id=1, source_target_pairs={{0,8},{8,16},{16,24},{24,32},{32,40},{40,48},{48,56},{56,0},{1,9},... | collective-permute-start | bytes 933896 | tf_op jit(solution)/shard_map/ppermute | solution.py:471
  11.5 3.9 %collective-permute-start.7 = (f32[608,128]{1,0:T(8,128)S(1)}, f32[608,128]{1,0:T(8,128)S(1)}, u32[]{:S(2)}, u32[]{:S(2)}) collective-permute-start(f32[608,128]{1,0:T(8,128)S(1)} %get-tuple-element.25), channel_id=1, source_target_pairs={{0,56},{8,0},{16,8},{24,16},{32,24},{40,32},{48,40},{56,48},{1,57}... | collective-permute-start | bytes 933896 | tf_op jit(solution)/shard_map/ppermute | solution.py:471
  15.4 0.0 collective-permute-done.4.sprev
  15.5 2.9 %collective-permute-start.5 = (f32[128,128]{1,0:T(8,128)S(1)}, f32[128,128]{1,0:T(8,128)S(1)}, u32[]{:S(2)}, u32[]{:S(2)}) collective-permute-start(f32[128,128]{1,0:T(8,128)S(1)} %get-tuple-element.22), channel_id=1, source_target_pairs={{0,192},{64,0},{128,64},{192,128},{1,193},{65,1},{129,65},{193,129... | collective-permute-start | bytes 196616 | tf_op jit(solution)/shard_map/ppermute | solution.py:471
  18.3 1.9 %collective-permute-done.5.snext = f32[128,128]{1,0:T(8,128)S(1)} collective-permute-done((f32[128,128]{1,0:T(8,128)S(1)}, f32[128,128]{1,0:T(8,128)S(1)}, u32[]{:S(2)}, u32[]{:S(2)}) %collective-permute-start.5) | collective-permute-done | bytes 65568 | tf_op jit(solution)/shard_map/ppermute | solution.py:471
  20.2 0.0 collective-permute-done.2.xprev
  20.2 0.0 collective-permute-done.3.xnext
  20.2 0.1 shard_map.52
  20.4 0.7 %collective-permute-start.8 = (f32[384,128]{1,0:T(8,128)S(1)}, f32[384,128]{1,0:T(8,128)S(1)}, u32[]{:S(2)}, u32[]{:S(2)}) collective-permute-start(f32[384,128]{1,0:T(8,128)S(1)} %get-tuple-element.26), channel_id=1, source_target_pairs={{0,8},{8,16},{16,24},{24,32},{32,40},{40,48},{48,56},{56,0},{1,9},... | collective-permute-start | bytes 589832 | tf_op jit(solution)/shard_map/ppermute | solution.py:471
  21.1 4.2 %collective-permute-start.9 = (f32[384,128]{1,0:T(8,128)S(1)}, f32[384,128]{1,0:T(8,128)S(1)}, u32[]{:S(2)}, u32[]{:S(2)}) collective-permute-start(f32[384,128]{1,0:T(8,128)S(1)} %get-tuple-element.27), channel_id=1, source_target_pairs={{0,56},{8,0},{16,8},{24,16},{32,24},{40,32},{48,40},{56,48},{1,57}... | collective-permute-start | bytes 589832 | tf_op jit(solution)/shard_map/ppermute | solution.py:471
  25.3 0.0 collective-permute-done.6.prev
  25.3 0.0 collective-permute-done.7.nxt
  25.4 3.3 %collective-permute-done.8.eprev = f32[384,128]{1,0:T(8,128)S(1)} collective-permute-done((f32[384,128]{1,0:T(8,128)S(1)}, f32[384,128]{1,0:T(8,128)S(1)}, u32[]{:S(2)}, u32[]{:S(2)}) %collective-permute-start.8) | collective-permute-done | bytes 196640 | tf_op jit(solution)/shard_map/ppermute | solution.py:471
  28.7 0.0 collective-permute-done.9.enext
  28.7 8.8 %shard_map.54 = (f32[5120,128]{1,0:T(8,128)S(1)}, f32[32,128]{1,0:T(8,128)S(1)}) custom-call(f32[1280,128]{1,0:T(8,128)S(1)} %bitcast.5, f32[256,128]{1,0:T(8,128)S(1)} %get-tuple-element.18.slabs, f32[1216,128]{1,0:T(8,128)S(1)} %get-tuple-element.23.kept, f32[128,128]{1,0:T(8,128)S(1)} %collective-permute-done.4.sprev, ...), custom_call_target="tpu_custom_call" | custom-call | tf_op jit(solution)/shard_map/pallas_call | solution.py:459
  37.5 0.0 collective-permute-start.10
  37.6 1.2 %collective-permute-done.10 = f32[32,128]{1,0:T(8,128)S(1)} collective-permute-done((f32[32,128]{1,0:T(8,128)S(1)}, f32[32,128]{1,0:T(8,128)S(1)}, u32[]{:S(2)}, u32[]{:S(2)}) %collective-permute-start.10) | collective-permute-done | bytes 16416 | tf_op jit(solution)/shard_map/ppermute | solution.py:471
  38.8 14.4 %all_to_all.10 = f32[16,32,128]{2,1,0:T(8,128)S(1)} all-to-all(f32[16,32,128]{2,1,0:T(8,128)S(1)} %broadcast_in_dim.7), channel_id=1, replica_groups=mesh['gx'=4,'gy'=8,'zx'=4,'core'=2] {'gx','zx'}, dimensions={0} | all-to-all | bytes 524288 | tf_op jit(solution)/shard_map/all_to_all | solution.py:476
  53.2 14.8 %all_to_all.11.parts = f32[8,32,128]{2,1,0:T(8,128)S(1)} all-to-all(f32[8,32,128]{2,1,0:T(8,128)S(1)} %broadcast_in_dim.8), channel_id=1, replica_groups=mesh['gx'=4,'gy'=8,'zx'=4,'core'=2] {'gy'}, dimensions={0} | all-to-all | bytes 262144 | tf_op jit(solution)/shard_map/all_to_all | solution.py:476
  68.0 4.5 %shard_map.55 = (f32[16,64,128]{2,1,0:T(8,128)}, f32[16,64,128]{2,1,0:T(8,128)}) custom-call(f32[8,32,128]{2,1,0:T(8,128)S(1)} %all_to_all.11.parts, f32[5120,128]{1,0:T(8,128)S(1)} %get-tuple-element.29.basis), custom_call_target="tpu_custom_call" | custom-call | tf_op jit(solution)/shard_map/pallas_call | solution.py:459
  (6 shorter events, 0.1 us)
Async XLA Ops:
  2.1 18.1 %collective-permute-start.2 = (f32[608,128]{1,0:T(8,128)S(1)}, f32[608,128]{1,0:T(8,128)S(1)}, u32[]{:S(2)}, u32[]{:S(2)}) collective-permute-start(f32[608,128]{1,0:T(8,128)S(1)} %get-tuple-element.19), channel_id=1, source_target_pairs={{0,64},{64,128},{128,192},{192,0},{1,65},{65,129},{129,193},{193,1... | collective-permute-start | bytes 933896 | tf_op jit(solution)/shard_map/ppermute | solution.py:471
  3.8 16.5 %collective-permute-start.3 = (f32[608,128]{1,0:T(8,128)S(1)}, f32[608,128]{1,0:T(8,128)S(1)}, u32[]{:S(2)}, u32[]{:S(2)}) collective-permute-start(f32[608,128]{1,0:T(8,128)S(1)} %get-tuple-element.20), channel_id=1, source_target_pairs={{0,192},{64,0},{128,64},{192,128},{1,193},{65,1},{129,65},{193,129... | collective-permute-start | bytes 933896 | tf_op jit(solution)/shard_map/ppermute | solution.py:471
  5.4 3.7 %collective-permute-start.1 = (f32[128,128]{1,0:T(8,128)S(1)}, f32[128,128]{1,0:T(8,128)S(1)}, u32[]{:S(2)}, u32[]{:S(2)}) collective-permute-start(f32[128,128]{1,0:T(8,128)S(1)} %get-tuple-element.17.ends), channel_id=1, source_target_pairs={{1,2},{3,4},{5,6},{7,0},{2,1},{4,3},{6,5},{0,7},{9,10},{11,12},{13... | collective-permute-start | bytes 196616 | tf_op jit(solution)/shard_map/ppermute | solution.py:488
  5.4 3.7 %collective-permute-start = (f32[128,128]{1,0:T(8,128)S(1)}, f32[128,128]{1,0:T(8,128)S(1)}, u32[]{:S(2)}, u32[]{:S(2)}) collective-permute-start(f32[128,128]{1,0:T(8,128)S(1)} %get-tuple-element.17.ends), channel_id=1, source_target_pairs={{0,1},{1,0},{2,3},{3,2},{4,5},{5,4},{6,7},{7,6},{8,9},{9,8},{10,11... | collective-permute-start | bytes 196616 | tf_op jit(solution)/shard_map/ppermute | solution.py:486
  9.1 6.3 %collective-permute-start.4 = (f32[128,128]{1,0:T(8,128)S(1)}, f32[128,128]{1,0:T(8,128)S(1)}, u32[]{:S(2)}, u32[]{:S(2)}) collective-permute-start(f32[128,128]{1,0:T(8,128)S(1)} %get-tuple-element.21), channel_id=1, source_target_pairs={{0,64},{64,128},{128,192},{192,0},{1,65},{65,129},{129,193},{193,1... | collective-permute-start | bytes 196616 | tf_op jit(solution)/shard_map/ppermute | solution.py:471
  9.6 15.7 %collective-permute-start.6 = (f32[608,128]{1,0:T(8,128)S(1)}, f32[608,128]{1,0:T(8,128)S(1)}, u32[]{:S(2)}, u32[]{:S(2)}) collective-permute-start(f32[608,128]{1,0:T(8,128)S(1)} %get-tuple-element.24), channel_id=1, source_target_pairs={{0,8},{8,16},{16,24},{24,32},{32,40},{40,48},{48,56},{56,0},{1,9},... | collective-permute-start | bytes 933896 | tf_op jit(solution)/shard_map/ppermute | solution.py:471
  11.5 13.8 %collective-permute-start.7 = (f32[608,128]{1,0:T(8,128)S(1)}, f32[608,128]{1,0:T(8,128)S(1)}, u32[]{:S(2)}, u32[]{:S(2)}) collective-permute-start(f32[608,128]{1,0:T(8,128)S(1)} %get-tuple-element.25), channel_id=1, source_target_pairs={{0,56},{8,0},{16,8},{24,16},{32,24},{40,32},{48,40},{56,48},{1,57}... | collective-permute-start | bytes 933896 | tf_op jit(solution)/shard_map/ppermute | solution.py:471
  15.5 4.8 %collective-permute-start.5 = (f32[128,128]{1,0:T(8,128)S(1)}, f32[128,128]{1,0:T(8,128)S(1)}, u32[]{:S(2)}, u32[]{:S(2)}) collective-permute-start(f32[128,128]{1,0:T(8,128)S(1)} %get-tuple-element.22), channel_id=1, source_target_pairs={{0,192},{64,0},{128,64},{192,128},{1,193},{65,1},{129,65},{193,129... | collective-permute-start | bytes 196616 | tf_op jit(solution)/shard_map/ppermute | solution.py:471
  20.4 8.3 %collective-permute-start.8 = (f32[384,128]{1,0:T(8,128)S(1)}, f32[384,128]{1,0:T(8,128)S(1)}, u32[]{:S(2)}, u32[]{:S(2)}) collective-permute-start(f32[384,128]{1,0:T(8,128)S(1)} %get-tuple-element.26), channel_id=1, source_target_pairs={{0,8},{8,16},{16,24},{24,32},{32,40},{40,48},{48,56},{56,0},{1,9},... | collective-permute-start | bytes 589832 | tf_op jit(solution)/shard_map/ppermute | solution.py:471
  21.1 7.6 %collective-permute-start.9 = (f32[384,128]{1,0:T(8,128)S(1)}, f32[384,128]{1,0:T(8,128)S(1)}, u32[]{:S(2)}, u32[]{:S(2)}) collective-permute-start(f32[384,128]{1,0:T(8,128)S(1)} %get-tuple-element.27), channel_id=1, source_target_pairs={{0,56},{8,0},{16,8},{24,16},{32,24},{40,32},{48,40},{56,48},{1,57}... | collective-permute-start | bytes 589832 | tf_op jit(solution)/shard_map/ppermute | solution.py:471
  37.5 1.2 %collective-permute-start.10 = (f32[32,128]{1,0:T(8,128)S(1)}, f32[32,128]{1,0:T(8,128)S(1)}, u32[]{:S(2)}, u32[]{:S(2)}) collective-permute-start(f32[32,128]{1,0:T(8,128)S(1)} %get-tuple-element.28), channel_id=1, source_target_pairs={{0,1},{1,0},{2,3},{3,2},{4,5},{5,4},{6,7},{7,6},{8,9},{9,8},{10,11... | collective-permute-start | bytes 49160 | tf_op jit(solution)/shard_map/ppermute | solution.py:471

commit v2 on v1

--- a/solution.py
+++ b/solution.py
@@ -92,7 +92,7 @@
 COEF_AT = RHS * 12
 ENDS_AT = ((COEF_AT + 24, EDGES3), (COEF_AT + 30, EDGES2), (COEF_AT + 32, EDGES2), (COEF_AT + 34, ()))
 FACE_AT = (COEF_AT + 34, COEF_AT + 58, COEF_AT + 74, COEF_AT + 90)
-EDGE_ROWS = 384
+EDGE_ROWS = 296
 
 
 def pack_edges(slabs, xprev, xnext, sprev, snext, ylow, yhigh, kept):
@@ -491,6 +491,7 @@
     )
     sprev = shift(shigh, "gx", 1)
     snext = shift(slow, "gx", -1)
+    ylow, sprev, snext = lax.optimization_barrier((ylow, sprev, snext))
     yprev = shift(yhigh, "gy", 1)
     ynext = shift(ylow, "gy", -1)
     edge = (EDGE_ROWS, 128)

time: 72.9 us -> 74.4 us (1.021)
  transfers between devices with their start and end apart: 11 -> 11, of which waited for: 4 -> 7; matrix products, arithmetic and copies ran while one was open for 0% -> 0% of each run, Pallas kernels for 0% -> 0%
where the time goes in v2:
time: 74.4 us; the launch traced here: 74.2 us
  blocking collectives  29.8 us (40%)
  starting transfers between devices  19.4 us (26%)
  Pallas kernels  13.8 us (19%)
  waiting for transfers between devices  9.13 us (12%)
  other arithmetic  1.19 us (2%)
  between operations  0.87 us (1%)
    all_to_all x2, blocking collectives, gathered(): lax.all_to_all(jnp.broadcast_to(value[None], (count,) + value.shape), axi...  29.8 us
    ppermute x9, starting transfers between devices, shift(): lax.ppermute(value, axis, [(i, (i + by) % count) for i in range(count)])  17.7 us
    pallas_call x6, Pallas kernels, call(): pl.pallas_call(kernel, out_shape=[jax.ShapeDtypeStruct(s, F32) for s in o...  13.8 us
    ppermute x9, waiting for transfers between devices, shift(): lax.ppermute(value, axis, [(i, (i + by) % count) for i in range(count)])  7.04 us
    ppermute x1, waiting for transfers between devices, shards(): lax.ppermute(ends_z, ('zx', 'core'), pairs + [(b, a) for a, b in pairs])  2.08 us
    ppermute x1, starting transfers between devices, shards(): lax.ppermute(ends_z, ('zx', 'core'), [(i, i ^ 1) for i in range(count)])  1.6 us
  transfers between devices with their start and end apart: 11, of which 7 were waited for; matrix products, arithmetic and copies ran while one was open for 0% of the time, Pallas kernels for 0%

profile of v2, /device:TPU:2, one launch (start us, length us, event | category | flops | bytes accessed | tf_op | source)
XLA Modules:
  0.0 74.2 jit_solution(17521177411415570326)
XLA Ops:
  0.6 1.2 %pad_maximum_fusion = f32[20,8,8,128]{3,2,1,0:T(8,128)S(1)} fusion(f32[3,8,8,128]{3,2,1,0:T(8,128)} %param.5, f32[1,8,8,128]{3,2,1,0:T(8,128)} %bitcast.6, f32[16,8,8,128]{3,2,1,0:T(8,128)} %param.3), kind=kLoop, calls=%fused_computation | loop fusion | flops 327680 | bytes 1310720 | tf_op jit(solution)/shard_map/concatenate | solution.py:480
  1.8 0.3 shard_map.50
  2.1 1.7 %collective-permute-start.2 = (f32[608,128]{1,0:T(8,128)S(1)}, f32[608,128]{1,0:T(8,128)S(1)}, u32[]{:S(2)}, u32[]{:S(2)}) collective-permute-start(f32[608,128]{1,0:T(8,128)S(1)} %get-tuple-element.22), channel_id=1, source_target_pairs={{0,64},{64,128},{128,192},{192,0},{1,65},{65,129},{129,193},{193,1... | collective-permute-start | bytes 933896 | tf_op jit(solution)/shard_map/ppermute | solution.py:471
  3.8 1.7 %collective-permute-start.3 = (f32[608,128]{1,0:T(8,128)S(1)}, f32[608,128]{1,0:T(8,128)S(1)}, u32[]{:S(2)}, u32[]{:S(2)}) collective-permute-start(f32[608,128]{1,0:T(8,128)S(1)} %get-tuple-element.23), channel_id=1, source_target_pairs={{0,192},{64,0},{128,64},{192,128},{1,193},{65,1},{129,65},{193,129... | collective-permute-start | bytes 933896 | tf_op jit(solution)/shard_map/ppermute | solution.py:471
  5.4 0.0 collective-permute-start.1
  5.4 1.6 %collective-permute-start = (f32[128,128]{1,0:T(8,128)S(1)}, f32[128,128]{1,0:T(8,128)S(1)}, u32[]{:S(2)}, u32[]{:S(2)}) collective-permute-start(f32[128,128]{1,0:T(8,128)S(1)} %get-tuple-element.20.ends), channel_id=1, source_target_pairs={{0,1},{1,0},{2,3},{3,2},{4,5},{5,4},{6,7},{7,6},{8,9},{9,8},{10,11... | collective-permute-start | bytes 196616 | tf_op jit(solution)/shard_map/ppermute | solution.py:486
  7.0 2.1 %collective-permute-done.1.other = f32[128,128]{1,0:T(8,128)S(1)} collective-permute-done((f32[128,128]{1,0:T(8,128)S(1)}, f32[128,128]{1,0:T(8,128)S(1)}, u32[]{:S(2)}, u32[]{:S(2)}) %collective-permute-start.1) | collective-permute-done | bytes 65568 | tf_op jit(solution)/shard_map/ppermute | solution.py:488
  9.1 0.0 collective-permute-done.mate
  9.1 0.4 collective-permute-start.4
  9.6 2.9 %collective-permute-start.5 = (f32[128,128]{1,0:T(8,128)S(1)}, f32[128,128]{1,0:T(8,128)S(1)}, u32[]{:S(2)}, u32[]{:S(2)}) collective-permute-start(f32[128,128]{1,0:T(8,128)S(1)} %get-tuple-element.26), channel_id=1, source_target_pairs={{0,192},{64,0},{128,64},{192,128},{1,193},{65,1},{129,65},{193,129... | collective-permute-start | bytes 196616 | tf_op jit(solution)/shard_map/ppermute | solution.py:471
  12.5 1.9 %collective-permute-start.6 = (f32[608,128]{1,0:T(8,128)S(1)}, f32[608,128]{1,0:T(8,128)S(1)}, u32[]{:S(2)}, u32[]{:S(2)}) collective-permute-start(f32[608,128]{1,0:T(8,128)S(1)} %get-tuple-element.30), channel_id=1, source_target_pairs={{0,8},{8,16},{16,24},{24,32},{32,40},{40,48},{48,56},{56,0},{1,9},... | collective-permute-start | bytes 933896 | tf_op jit(solution)/shard_map/ppermute | solution.py:471
  14.4 0.3 collective-permute-done.4.sprev
  14.7 0.0 collective-permute-done.5.snext
  14.7 5.9 %collective-permute-start.7 = (f32[608,128]{1,0:T(8,128)S(1)}, f32[608,128]{1,0:T(8,128)S(1)}, u32[]{:S(2)}, u32[]{:S(2)}) collective-permute-start(f32[608,128]{1,0:T(8,128)S(1)} %get-tuple-element.31), channel_id=1, source_target_pairs={{0,56},{8,0},{16,8},{24,16},{32,24},{40,32},{48,40},{56,48},{1,57}... | collective-permute-start | bytes 933896 | tf_op jit(solution)/shard_map/ppermute | solution.py:471
  20.6 0.0 collective-permute-done.2.xprev
  20.6 0.0 collective-permute-done.3.xnext
  20.6 0.1 shard_map.52
  20.7 0.1 collective-permute-start.8
  20.8 3.2 %collective-permute-start.9 = (f32[296,128]{1,0:T(8,128)S(1)}, f32[296,128]{1,0:T(8,128)S(1)}, u32[]{:S(2)}, u32[]{:S(2)}) collective-permute-start(f32[296,128]{1,0:T(8,128)S(1)} %get-tuple-element.33), channel_id=1, source_target_pairs={{0,56},{8,0},{16,8},{24,16},{32,24},{40,32},{48,40},{56,48},{1,57}... | collective-permute-start | bytes 454664 | tf_op jit(solution)/shard_map/ppermute | solution.py:471
  24.0 2.5 %collective-permute-done.6.prev = f32[608,128]{1,0:T(8,128)S(1)} collective-permute-done((f32[608,128]{1,0:T(8,128)S(1)}, f32[608,128]{1,0:T(8,128)S(1)}, u32[]{:S(2)}, u32[]{:S(2)}) %collective-permute-start.6) | collective-permute-done | bytes 311328 | tf_op jit(solution)/shard_map/ppermute | solution.py:471
  26.5 1.4 %collective-permute-done.7.nxt = f32[608,128]{1,0:T(8,128)S(1)} collective-permute-done((f32[608,128]{1,0:T(8,128)S(1)}, f32[608,128]{1,0:T(8,128)S(1)}, u32[]{:S(2)}, u32[]{:S(2)}) %collective-permute-start.7) | collective-permute-done | bytes 311328 | tf_op jit(solution)/shard_map/ppermute | solution.py:471
  28.0 0.7 collective-permute-done.8.eprev
  28.7 0.9 %collective-permute-done.9.enext = f32[296,128]{1,0:T(8,128)S(1)} collective-permute-done((f32[296,128]{1,0:T(8,128)S(1)}, f32[296,128]{1,0:T(8,128)S(1)}, u32[]{:S(2)}, u32[]{:S(2)}) %collective-permute-start.9) | collective-permute-done | bytes 151584 | tf_op jit(solution)/shard_map/ppermute | solution.py:471
  29.6 8.8 %shard_map.54 = (f32[5120,128]{1,0:T(8,128)S(1)}, f32[32,128]{1,0:T(8,128)S(1)}) custom-call(f32[1280,128]{1,0:T(8,128)S(1)} %bitcast.5, f32[256,128]{1,0:T(8,128)S(1)} %get-tuple-element.21.slabs, f32[1216,128]{1,0:T(8,128)S(1)} %get-tuple-element.29.kept, f32[128,128]{1,0:T(8,128)S(1)} %collective-permute-done.4.sprev, ...), custom_call_target="tpu_custom_call" | custom-call | tf_op jit(solution)/shard_map/pallas_call | solution.py:459
  38.4 0.0 collective-permute-start.10
  38.5 1.2 %collective-permute-done.10 = f32[32,128]{1,0:T(8,128)S(1)} collective-permute-done((f32[32,128]{1,0:T(8,128)S(1)}, f32[32,128]{1,0:T(8,128)S(1)}, u32[]{:S(2)}, u32[]{:S(2)}) %collective-permute-start.10) | collective-permute-done | bytes 16416 | tf_op jit(solution)/shard_map/ppermute | solution.py:471
  39.7 15.9 %all_to_all.10 = f32[16,32,128]{2,1,0:T(8,128)S(1)} all-to-all(f32[16,32,128]{2,1,0:T(8,128)S(1)} %broadcast_in_dim.7), channel_id=1, replica_groups=mesh['gx'=4,'gy'=8,'zx'=4,'core'=2] {'gx','zx'}, dimensions={0} | all-to-all | bytes 524288 | tf_op jit(solution)/shard_map/all_to_all | solution.py:476
  55.6 14.0 %all_to_all.11.parts = f32[8,32,128]{2,1,0:T(8,128)S(1)} all-to-all(f32[8,32,128]{2,1,0:T(8,128)S(1)} %broadcast_in_dim.8), channel_id=1, replica_groups=mesh['gx'=4,'gy'=8,'zx'=4,'core'=2] {'gy'}, dimensions={0} | all-to-all | bytes 262144 | tf_op jit(solution)/shard_map/all_to_all | solution.py:476
  69.6 4.5 %shard_map.55 = (f32[16,64,128]{2,1,0:T(8,128)}, f32[16,64,128]{2,1,0:T(8,128)}) custom-call(f32[8,32,128]{2,1,0:T(8,128)S(1)} %all_to_all.11.parts, f32[5120,128]{1,0:T(8,128)S(1)} %get-tuple-element.35.basis), custom_call_target="tpu_custom_call" | custom-call | tf_op jit(solution)/shard_map/pallas_call | solution.py:459
  (6 shorter events, 0.1 us)
Async XLA Ops:
  2.1 18.4 %collective-permute-start.2 = (f32[608,128]{1,0:T(8,128)S(1)}, f32[608,128]{1,0:T(8,128)S(1)}, u32[]{:S(2)}, u32[]{:S(2)}) collective-permute-start(f32[608,128]{1,0:T(8,128)S(1)} %get-tuple-element.22), channel_id=1, source_target_pairs={{0,64},{64,128},{128,192},{192,0},{1,65},{65,129},{129,193},{193,1... | collective-permute-start | bytes 933896 | tf_op jit(solution)/shard_map/ppermute | solution.py:471
  3.8 16.8 %collective-permute-start.3 = (f32[608,128]{1,0:T(8,128)S(1)}, f32[608,128]{1,0:T(8,128)S(1)}, u32[]{:S(2)}, u32[]{:S(2)}) collective-permute-start(f32[608,128]{1,0:T(8,128)S(1)} %get-tuple-element.23), channel_id=1, source_target_pairs={{0,192},{64,0},{128,64},{192,128},{1,193},{65,1},{129,65},{193,129... | collective-permute-start | bytes 933896 | tf_op jit(solution)/shard_map/ppermute | solution.py:471
  5.4 3.7 %collective-permute-start.1 = (f32[128,128]{1,0:T(8,128)S(1)}, f32[128,128]{1,0:T(8,128)S(1)}, u32[]{:S(2)}, u32[]{:S(2)}) collective-permute-start(f32[128,128]{1,0:T(8,128)S(1)} %get-tuple-element.20.ends), channel_id=1, source_target_pairs={{1,2},{3,4},{5,6},{7,0},{2,1},{4,3},{6,5},{0,7},{9,10},{11,12},{13... | collective-permute-start | bytes 196616 | tf_op jit(solution)/shard_map/ppermute | solution.py:488
  5.4 3.7 %collective-permute-start = (f32[128,128]{1,0:T(8,128)S(1)}, f32[128,128]{1,0:T(8,128)S(1)}, u32[]{:S(2)}, u32[]{:S(2)}) collective-permute-start(f32[128,128]{1,0:T(8,128)S(1)} %get-tuple-element.20.ends), channel_id=1, source_target_pairs={{0,1},{1,0},{2,3},{3,2},{4,5},{5,4},{6,7},{7,6},{8,9},{9,8},{10,11... | collective-permute-start | bytes 196616 | tf_op jit(solution)/shard_map/ppermute | solution.py:486
  9.1 5.6 %collective-permute-start.4 = (f32[128,128]{1,0:T(8,128)S(1)}, f32[128,128]{1,0:T(8,128)S(1)}, u32[]{:S(2)}, u32[]{:S(2)}) collective-permute-start(f32[128,128]{1,0:T(8,128)S(1)} %get-tuple-element.25), channel_id=1, source_target_pairs={{0,64},{64,128},{128,192},{192,0},{1,65},{65,129},{129,193},{193,1... | collective-permute-start | bytes 196616 | tf_op jit(solution)/shard_map/ppermute | solution.py:471
  9.6 5.1 %collective-permute-start.5 = (f32[128,128]{1,0:T(8,128)S(1)}, f32[128,128]{1,0:T(8,128)S(1)}, u32[]{:S(2)}, u32[]{:S(2)}) collective-permute-start(f32[128,128]{1,0:T(8,128)S(1)} %get-tuple-element.26), channel_id=1, source_target_pairs={{0,192},{64,0},{128,64},{192,128},{1,193},{65,1},{129,65},{193,129... | collective-permute-start | bytes 196616 | tf_op jit(solution)/shard_map/ppermute | solution.py:471
  12.5 14.1 %collective-permute-start.6 = (f32[608,128]{1,0:T(8,128)S(1)}, f32[608,128]{1,0:T(8,128)S(1)}, u32[]{:S(2)}, u32[]{:S(2)}) collective-permute-start(f32[608,128]{1,0:T(8,128)S(1)} %get-tuple-element.30), channel_id=1, source_target_pairs={{0,8},{8,16},{16,24},{24,32},{32,40},{40,48},{48,56},{56,0},{1,9},... | collective-permute-start | bytes 933896 | tf_op jit(solution)/shard_map/ppermute | solution.py:471
  14.7 13.3 %collective-permute-start.7 = (f32[608,128]{1,0:T(8,128)S(1)}, f32[608,128]{1,0:T(8,128)S(1)}, u32[]{:S(2)}, u32[]{:S(2)}) collective-permute-start(f32[608,128]{1,0:T(8,128)S(1)} %get-tuple-element.31), channel_id=1, source_target_pairs={{0,56},{8,0},{16,8},{24,16},{32,24},{40,32},{48,40},{56,48},{1,57}... | collective-permute-start | bytes 933896 | tf_op jit(solution)/shard_map/ppermute | solution.py:471
  20.7 8.0 %collective-permute-start.8 = (f32[296,128]{1,0:T(8,128)S(1)}, f32[296,128]{1,0:T(8,128)S(1)}, u32[]{:S(2)}, u32[]{:S(2)}) collective-permute-start(f32[296,128]{1,0:T(8,128)S(1)} %get-tuple-element.32), channel_id=1, source_target_pairs={{0,8},{8,16},{16,24},{24,32},{32,40},{40,48},{48,56},{56,0},{1,9},... | collective-permute-start | bytes 454664 | tf_op jit(solution)/shard_map/ppermute | solution.py:471
  20.8 8.8 %collective-permute-start.9 = (f32[296,128]{1,0:T(8,128)S(1)}, f32[296,128]{1,0:T(8,128)S(1)}, u32[]{:S(2)}, u32[]{:S(2)}) collective-permute-start(f32[296,128]{1,0:T(8,128)S(1)} %get-tuple-element.33), channel_id=1, source_target_pairs={{0,56},{8,0},{16,8},{24,16},{32,24},{40,32},{48,40},{56,48},{1,57}... | collective-permute-start | bytes 454664 | tf_op jit(solution)/shard_map/ppermute | solution.py:471
  38.4 1.2 %collective-permute-start.10 = (f32[32,128]{1,0:T(8,128)S(1)}, f32[32,128]{1,0:T(8,128)S(1)}, u32[]{:S(2)}, u32[]{:S(2)}) collective-permute-start(f32[32,128]{1,0:T(8,128)S(1)} %get-tuple-element.34), channel_id=1, source_target_pairs={{0,1},{1,0},{2,3},{3,2},{4,5},{5,4},{6,7},{7,6},{8,9},{9,8},{10,11... | collective-permute-start | bytes 49160 | tf_op jit(solution)/shard_map/ppermute | solution.py:471

commit v3 on v2

--- a/solution.py
+++ b/solution.py
@@ -491,7 +491,6 @@
     )
     sprev = shift(shigh, "gx", 1)
     snext = shift(slow, "gx", -1)
-    ylow, sprev, snext = lax.optimization_barrier((ylow, sprev, snext))
     yprev = shift(yhigh, "gy", 1)
     ynext = shift(ylow, "gy", -1)
     edge = (EDGE_ROWS, 128)

time: 74.4 us -> 73.3 us (0.985)
  waiting for transfers between devices: 9.13 us -> 13.2 us
  blocking collectives: 29.8 us -> 26.9 us
  starting transfers between devices: 19.4 us -> 17.1 us
    ppermute x9, waiting for transfers between devices: 7.04 us -> 13.1 us  [shift(): lax.ppermute(value, axis, [(i, (i + by) % count) for i in range(count)])]
    all_to_all x2, blocking collectives: 29.8 us -> 26.9 us  [gathered(): lax.all_to_all(jnp.broadcast_to(value[None], (count,) + value.shape), axi...]
    ppermute x9, starting transfers between devices: 17.7 us -> 15.5 us  [shift(): lax.ppermute(value, axis, [(i, (i + by) % count) for i in range(count)])]
    ppermute x1, waiting for transfers between devices: 2.08 us -> 0.17 us  [shards(): lax.ppermute(ends_z, ('zx', 'core'), pairs + [(b, a) for a, b in pairs])]
  transfers between devices with their start and end apart: 11 -> 11, of which waited for: 7 -> 5; matrix products, arithmetic and copies ran while one was open for 0% -> 0% of each run, Pallas kernels for 0% -> 0%
where the time goes in v3:
time: 73.3 us; the launch traced here: 73.2 us
  blocking collectives  26.9 us (37%)
  starting transfers between devices  17.1 us (23%)
  Pallas kernels  13.8 us (19%)
  waiting for transfers between devices  13.2 us (18%)
  other arithmetic  1.19 us (2%)
  between operations  0.87 us (1%)
    all_to_all x2, blocking collectives, gathered(): lax.all_to_all(jnp.broadcast_to(value[None], (count,) + value.shape), axi...  26.9 us
    ppermute x9, starting transfers between devices, shift(): lax.ppermute(value, axis, [(i, (i + by) % count) for i in range(count)])  15.5 us
    pallas_call x6, Pallas kernels, call(): pl.pallas_call(kernel, out_shape=[jax.ShapeDtypeStruct(s, F32) for s in o...  13.8 us
    ppermute x9, waiting for transfers between devices, shift(): lax.ppermute(value, axis, [(i, (i + by) % count) for i in range(count)])  13.1 us
    ppermute x1, starting transfers between devices, shards(): lax.ppermute(ends_z, ('zx', 'core'), [(i, i ^ 1) for i in range(count)])  1.6 us
  transfers between devices with their start and end apart: 11, of which 5 were waited for; matrix products, arithmetic and copies ran while one was open for 0% of the time, Pallas kernels for 0%

profile of v3, /device:TPU:2, one launch (start us, length us, event | category | flops | bytes accessed | tf_op | source)
XLA Modules:
  0.0 73.2 jit_solution(13581779821881820452)
XLA Ops:
  0.6 1.2 %pad_maximum_fusion = f32[20,8,8,128]{3,2,1,0:T(8,128)S(1)} fusion(f32[3,8,8,128]{3,2,1,0:T(8,128)} %param.5, f32[1,8,8,128]{3,2,1,0:T(8,128)} %bitcast.6, f32[16,8,8,128]{3,2,1,0:T(8,128)} %param.3), kind=kLoop, calls=%fused_computation | loop fusion | flops 327680 | bytes 1310720 | tf_op jit(solution)/shard_map/concatenate | solution.py:480
  1.8 0.3 shard_map.50
  2.1 1.7 %collective-permute-start.2 = (f32[608,128]{1,0:T(8,128)S(1)}, f32[608,128]{1,0:T(8,128)S(1)}, u32[]{:S(2)}, u32[]{:S(2)}) collective-permute-start(f32[608,128]{1,0:T(8,128)S(1)} %get-tuple-element.19), channel_id=1, source_target_pairs={{0,64},{64,128},{128,192},{192,0},{1,65},{65,129},{129,193},{193,1... | collective-permute-start | bytes 933896 | tf_op jit(solution)/shard_map/ppermute | solution.py:471
  3.8 1.7 %collective-permute-start.3 = (f32[608,128]{1,0:T(8,128)S(1)}, f32[608,128]{1,0:T(8,128)S(1)}, u32[]{:S(2)}, u32[]{:S(2)}) collective-permute-start(f32[608,128]{1,0:T(8,128)S(1)} %get-tuple-element.20), channel_id=1, source_target_pairs={{0,192},{64,0},{128,64},{192,128},{1,193},{65,1},{129,65},{193,129... | collective-permute-start | bytes 933896 | tf_op jit(solution)/shard_map/ppermute | solution.py:471
  5.4 0.0 collective-permute-start.1
  5.4 1.6 %collective-permute-start = (f32[128,128]{1,0:T(8,128)S(1)}, f32[128,128]{1,0:T(8,128)S(1)}, u32[]{:S(2)}, u32[]{:S(2)}) collective-permute-start(f32[128,128]{1,0:T(8,128)S(1)} %get-tuple-element.17.ends), channel_id=1, source_target_pairs={{0,1},{1,0},{2,3},{3,2},{4,5},{5,4},{6,7},{7,6},{8,9},{9,8},{10,11... | collective-permute-start | bytes 196616 | tf_op jit(solution)/shard_map/ppermute | solution.py:486
  7.0 1.9 %collective-permute-start.6 = (f32[608,128]{1,0:T(8,128)S(1)}, f32[608,128]{1,0:T(8,128)S(1)}, u32[]{:S(2)}, u32[]{:S(2)}) collective-permute-start(f32[608,128]{1,0:T(8,128)S(1)} %get-tuple-element.24), channel_id=1, source_target_pairs={{0,8},{8,16},{16,24},{24,32},{32,40},{40,48},{48,56},{56,0},{1,9},... | collective-permute-start | bytes 933896 | tf_op jit(solution)/shard_map/ppermute | solution.py:471
  9.0 0.2 collective-permute-done.1.other
  9.1 5.9 %collective-permute-start.7 = (f32[608,128]{1,0:T(8,128)S(1)}, f32[608,128]{1,0:T(8,128)S(1)}, u32[]{:S(2)}, u32[]{:S(2)}) collective-permute-start(f32[608,128]{1,0:T(8,128)S(1)} %get-tuple-element.25), channel_id=1, source_target_pairs={{0,56},{8,0},{16,8},{24,16},{32,24},{40,32},{48,40},{56,48},{1,57}... | collective-permute-start | bytes 933896 | tf_op jit(solution)/shard_map/ppermute | solution.py:471
  15.0 0.0 collective-permute-done.mate
  15.0 0.4 collective-permute-start.4
  15.4 5.1 %collective-permute-done.4.sprev = f32[128,128]{1,0:T(8,128)S(1)} collective-permute-done((f32[128,128]{1,0:T(8,128)S(1)}, f32[128,128]{1,0:T(8,128)S(1)}, u32[]{:S(2)}, u32[]{:S(2)}) %collective-permute-start.4) | collective-permute-done | bytes 65568 | tf_op jit(solution)/shard_map/ppermute | solution.py:471
  20.6 0.6 collective-permute-start.5
  21.2 3.7 %collective-permute-done.5.snext = f32[128,128]{1,0:T(8,128)S(1)} collective-permute-done((f32[128,128]{1,0:T(8,128)S(1)}, f32[128,128]{1,0:T(8,128)S(1)}, u32[]{:S(2)}, u32[]{:S(2)}) %collective-permute-start.5) | collective-permute-done | bytes 65568 | tf_op jit(solution)/shard_map/ppermute | solution.py:471
  24.8 0.0 collective-permute-done.2.xprev
  24.8 0.0 collective-permute-done.3.xnext
  24.8 0.1 shard_map.52
  25.0 0.1 collective-permute-start.8
  25.1 3.2 %collective-permute-start.9 = (f32[296,128]{1,0:T(8,128)S(1)}, f32[296,128]{1,0:T(8,128)S(1)}, u32[]{:S(2)}, u32[]{:S(2)}) collective-permute-start(f32[296,128]{1,0:T(8,128)S(1)} %get-tuple-element.27), channel_id=1, source_target_pairs={{0,56},{8,0},{16,8},{24,16},{32,24},{40,32},{48,40},{56,48},{1,57}... | collective-permute-start | bytes 454664 | tf_op jit(solution)/shard_map/ppermute | solution.py:471
  28.3 0.0 collective-permute-done.6.prev
  28.3 0.0 collective-permute-done.7.nxt
  28.3 3.1 %collective-permute-done.8.eprev = f32[296,128]{1,0:T(8,128)S(1)} collective-permute-done((f32[296,128]{1,0:T(8,128)S(1)}, f32[296,128]{1,0:T(8,128)S(1)}, u32[]{:S(2)}, u32[]{:S(2)}) %collective-permute-start.8) | collective-permute-done | bytes 151584 | tf_op jit(solution)/shard_map/ppermute | solution.py:471
  31.4 0.0 collective-permute-done.9.enext
  31.4 8.8 %shard_map.54 = (f32[5120,128]{1,0:T(8,128)S(1)}, f32[32,128]{1,0:T(8,128)S(1)}) custom-call(f32[1280,128]{1,0:T(8,128)S(1)} %bitcast.5, f32[256,128]{1,0:T(8,128)S(1)} %get-tuple-element.18.slabs, f32[1216,128]{1,0:T(8,128)S(1)} %get-tuple-element.23.kept, f32[128,128]{1,0:T(8,128)S(1)} %collective-permute-done.4.sprev, ...), custom_call_target="tpu_custom_call" | custom-call | tf_op jit(solution)/shard_map/pallas_call | solution.py:459
  40.3 0.0 collective-permute-start.10
  40.3 1.2 %collective-permute-done.10 = f32[32,128]{1,0:T(8,128)S(1)} collective-permute-done((f32[32,128]{1,0:T(8,128)S(1)}, f32[32,128]{1,0:T(8,128)S(1)}, u32[]{:S(2)}, u32[]{:S(2)}) %collective-permute-start.10) | collective-permute-done | bytes 16416 | tf_op jit(solution)/shard_map/ppermute | solution.py:471
  41.5 13.5 %all_to_all.10 = f32[16,32,128]{2,1,0:T(8,128)S(1)} all-to-all(f32[16,32,128]{2,1,0:T(8,128)S(1)} %broadcast_in_dim.7), channel_id=1, replica_groups=mesh['gx'=4,'gy'=8,'zx'=4,'core'=2] {'gx','zx'}, dimensions={0} | all-to-all | bytes 524288 | tf_op jit(solution)/shard_map/all_to_all | solution.py:476
  55.1 13.4 %all_to_all.11.parts = f32[8,32,128]{2,1,0:T(8,128)S(1)} all-to-all(f32[8,32,128]{2,1,0:T(8,128)S(1)} %broadcast_in_dim.8), channel_id=1, replica_groups=mesh['gx'=4,'gy'=8,'zx'=4,'core'=2] {'gy'}, dimensions={0} | all-to-all | bytes 262144 | tf_op jit(solution)/shard_map/all_to_all | solution.py:476
  68.5 4.5 %shard_map.55 = (f32[16,64,128]{2,1,0:T(8,128)}, f32[16,64,128]{2,1,0:T(8,128)}) custom-call(f32[8,32,128]{2,1,0:T(8,128)S(1)} %all_to_all.11.parts, f32[5120,128]{1,0:T(8,128)S(1)} %get-tuple-element.29.basis), custom_call_target="tpu_custom_call" | custom-call | tf_op jit(solution)/shard_map/pallas_call | solution.py:459
  (6 shorter events, 0.1 us)
Async XLA Ops:
  2.1 22.7 %collective-permute-start.2 = (f32[608,128]{1,0:T(8,128)S(1)}, f32[608,128]{1,0:T(8,128)S(1)}, u32[]{:S(2)}, u32[]{:S(2)}) collective-permute-start(f32[608,128]{1,0:T(8,128)S(1)} %get-tuple-element.19), channel_id=1, source_target_pairs={{0,64},{64,128},{128,192},{192,0},{1,65},{65,129},{129,193},{193,1... | collective-permute-start | bytes 933896 | tf_op jit(solution)/shard_map/ppermute | solution.py:471
  3.8 21.1 %collective-permute-start.3 = (f32[608,128]{1,0:T(8,128)S(1)}, f32[608,128]{1,0:T(8,128)S(1)}, u32[]{:S(2)}, u32[]{:S(2)}) collective-permute-start(f32[608,128]{1,0:T(8,128)S(1)} %get-tuple-element.20), channel_id=1, source_target_pairs={{0,192},{64,0},{128,64},{192,128},{1,193},{65,1},{129,65},{193,129... | collective-permute-start | bytes 933896 | tf_op jit(solution)/shard_map/ppermute | solution.py:471
  5.4 3.7 %collective-permute-start.1 = (f32[128,128]{1,0:T(8,128)S(1)}, f32[128,128]{1,0:T(8,128)S(1)}, u32[]{:S(2)}, u32[]{:S(2)}) collective-permute-start(f32[128,128]{1,0:T(8,128)S(1)} %get-tuple-element.17.ends), channel_id=1, source_target_pairs={{1,2},{3,4},{5,6},{7,0},{2,1},{4,3},{6,5},{0,7},{9,10},{11,12},{13... | collective-permute-start | bytes 196616 | tf_op jit(solution)/shard_map/ppermute | solution.py:488
  5.4 9.5 %collective-permute-start = (f32[128,128]{1,0:T(8,128)S(1)}, f32[128,128]{1,0:T(8,128)S(1)}, u32[]{:S(2)}, u32[]{:S(2)}) collective-permute-start(f32[128,128]{1,0:T(8,128)S(1)} %get-tuple-element.17.ends), channel_id=1, source_target_pairs={{0,1},{1,0},{2,3},{3,2},{4,5},{5,4},{6,7},{7,6},{8,9},{9,8},{10,11... | collective-permute-start | bytes 196616 | tf_op jit(solution)/shard_map/ppermute | solution.py:486
  7.0 21.2 %collective-permute-start.6 = (f32[608,128]{1,0:T(8,128)S(1)}, f32[608,128]{1,0:T(8,128)S(1)}, u32[]{:S(2)}, u32[]{:S(2)}) collective-permute-start(f32[608,128]{1,0:T(8,128)S(1)} %get-tuple-element.24), channel_id=1, source_target_pairs={{0,8},{8,16},{16,24},{24,32},{32,40},{40,48},{48,56},{56,0},{1,9},... | collective-permute-start | bytes 933896 | tf_op jit(solution)/shard_map/ppermute | solution.py:471
  9.1 19.2 %collective-permute-start.7 = (f32[608,128]{1,0:T(8,128)S(1)}, f32[608,128]{1,0:T(8,128)S(1)}, u32[]{:S(2)}, u32[]{:S(2)}) collective-permute-start(f32[608,128]{1,0:T(8,128)S(1)} %get-tuple-element.25), channel_id=1, source_target_pairs={{0,56},{8,0},{16,8},{24,16},{32,24},{40,32},{48,40},{56,48},{1,57}... | collective-permute-start | bytes 933896 | tf_op jit(solution)/shard_map/ppermute | solution.py:471
  15.0 5.6 %collective-permute-start.4 = (f32[128,128]{1,0:T(8,128)S(1)}, f32[128,128]{1,0:T(8,128)S(1)}, u32[]{:S(2)}, u32[]{:S(2)}) collective-permute-start(f32[128,128]{1,0:T(8,128)S(1)} %get-tuple-element.21), channel_id=1, source_target_pairs={{0,64},{64,128},{128,192},{192,0},{1,65},{65,129},{129,193},{193,1... | collective-permute-start | bytes 196616 | tf_op jit(solution)/shard_map/ppermute | solution.py:471
  20.6 4.3 %collective-permute-start.5 = (f32[128,128]{1,0:T(8,128)S(1)}, f32[128,128]{1,0:T(8,128)S(1)}, u32[]{:S(2)}, u32[]{:S(2)}) collective-permute-start(f32[128,128]{1,0:T(8,128)S(1)} %get-tuple-element.22), channel_id=1, source_target_pairs={{0,192},{64,0},{128,64},{192,128},{1,193},{65,1},{129,65},{193,129... | collective-permute-start | bytes 196616 | tf_op jit(solution)/shard_map/ppermute | solution.py:471
  25.0 6.5 %collective-permute-start.8 = (f32[296,128]{1,0:T(8,128)S(1)}, f32[296,128]{1,0:T(8,128)S(1)}, u32[]{:S(2)}, u32[]{:S(2)}) collective-permute-start(f32[296,128]{1,0:T(8,128)S(1)} %get-tuple-element.26), channel_id=1, source_target_pairs={{0,8},{8,16},{16,24},{24,32},{32,40},{40,48},{48,56},{56,0},{1,9},... | collective-permute-start | bytes 454664 | tf_op jit(solution)/shard_map/ppermute | solution.py:471
  25.1 6.4 %collective-permute-start.9 = (f32[296,128]{1,0:T(8,128)S(1)}, f32[296,128]{1,0:T(8,128)S(1)}, u32[]{:S(2)}, u32[]{:S(2)}) collective-permute-start(f32[296,128]{1,0:T(8,128)S(1)} %get-tuple-element.27), channel_id=1, source_target_pairs={{0,56},{8,0},{16,8},{24,16},{32,24},{40,32},{48,40},{56,48},{1,57}... | collective-permute-start | bytes 454664 | tf_op jit(solution)/shard_map/ppermute | solution.py:471
  40.3 1.2 %collective-permute-start.10 = (f32[32,128]{1,0:T(8,128)S(1)}, f32[32,128]{1,0:T(8,128)S(1)}, u32[]{:S(2)}, u32[]{:S(2)}) collective-permute-start(f32[32,128]{1,0:T(8,128)S(1)} %get-tuple-element.28), channel_id=1, source_target_pairs={{0,1},{1,0},{2,3},{3,2},{4,5},{5,4},{6,7},{7,6},{8,9},{9,8},{10,11... | collective-permute-start | bytes 49160 | tf_op jit(solution)/shard_map/ppermute | solution.py:471

commit v4 on v1

--- a/solution.py
+++ b/solution.py
@@ -12,7 +12,7 @@
 FILLS = 4
 MAKES = 7
 OWN = 8
-GRAMS = 16
+GRAMS = 32
 PAIRS = 8
 BLOCK = 4
 LOW = RHS * 512
@@ -284,8 +284,9 @@
 
         lax.fori_loop(0, 8 // OWN, inside, 0)
         if not last:
-            lax.fori_loop(0, 2, outside, 0)
-            lax.fori_loop(0, 2, halo, 0)
+            for half in range(2):
+                outside(half, 0)
+                halo(half, 0)
 
     zeros = jnp.zeros((128 - COLS, 256), BF16)
 

time: 72.9 us -> 71.6 us (0.982)
  Pallas kernels: 13.8 us -> 12.5 us
    pallas_call x6, Pallas kernels: 13.8 us -> 12.5 us  [call(): pl.pallas_call(kernel, out_shape=[jax.ShapeDtypeStruct(s, F32) for s in o...]
where the time goes in v4:
time: 71.6 us; the launch traced here: 71.4 us
  blocking collectives  29.2 us (41%)
  starting transfers between devices  19.1 us (27%)
  Pallas kernels  12.5 us (17%)
  waiting for transfers between devices  8.5 us (12%)
  other arithmetic  1.19 us (2%)
  between operations  0.86 us (1%)
    all_to_all x2, blocking collectives, gathered(): lax.all_to_all(jnp.broadcast_to(value[None], (count,) + value.shape), axi...  29.2 us
    ppermute x9, starting transfers between devices, shift(): lax.ppermute(value, axis, [(i, (i + by) % count) for i in range(count)])  17.5 us
    pallas_call x6, Pallas kernels, call(): pl.pallas_call(kernel, out_shape=[jax.ShapeDtypeStruct(s, F32) for s in o...  12.5 us
    ppermute x9, waiting for transfers between devices, shift(): lax.ppermute(value, axis, [(i, (i + by) % count) for i in range(count)])  6.42 us
    ppermute x1, waiting for transfers between devices, shards(): lax.ppermute(ends_z, ('zx', 'core'), pairs + [(b, a) for a, b in pairs])  2.08 us
    ppermute x1, starting transfers between devices, shards(): lax.ppermute(ends_z, ('zx', 'core'), [(i, i ^ 1) for i in range(count)])  1.6 us
  transfers between devices with their start and end apart: 11, of which 4 were waited for; matrix products, arithmetic and copies ran while one was open for 0% of the time, Pallas kernels for 0%

profile of v4, /device:TPU:2, one launch (start us, length us, event | category | flops | bytes accessed | tf_op | source)
XLA Modules:
  0.0 71.4 jit_solution(17263789266120750721)
XLA Ops:
  0.6 1.2 %pad_maximum_fusion = f32[20,8,8,128]{3,2,1,0:T(8,128)S(1)} fusion(f32[3,8,8,128]{3,2,1,0:T(8,128)} %param.5, f32[1,8,8,128]{3,2,1,0:T(8,128)} %bitcast.6, f32[16,8,8,128]{3,2,1,0:T(8,128)} %param.3), kind=kLoop, calls=%fused_computation | loop fusion | flops 327680 | bytes 1310720 | tf_op jit(solution)/shard_map/concatenate | solution.py:481
  1.8 0.3 shard_map.50
  2.1 1.7 %collective-permute-start.2 = (f32[608,128]{1,0:T(8,128)S(1)}, f32[608,128]{1,0:T(8,128)S(1)}, u32[]{:S(2)}, u32[]{:S(2)}) collective-permute-start(f32[608,128]{1,0:T(8,128)S(1)} %get-tuple-element.19), channel_id=1, source_target_pairs={{0,64},{64,128},{128,192},{192,0},{1,65},{65,129},{129,193},{193,1... | collective-permute-start | bytes 933896 | tf_op jit(solution)/shard_map/ppermute | solution.py:472
  3.8 1.7 %collective-permute-start.3 = (f32[608,128]{1,0:T(8,128)S(1)}, f32[608,128]{1,0:T(8,128)S(1)}, u32[]{:S(2)}, u32[]{:S(2)}) collective-permute-start(f32[608,128]{1,0:T(8,128)S(1)} %get-tuple-element.20), channel_id=1, source_target_pairs={{0,192},{64,0},{128,64},{192,128},{1,193},{65,1},{129,65},{193,129... | collective-permute-start | bytes 933896 | tf_op jit(solution)/shard_map/ppermute | solution.py:472
  5.4 0.0 collective-permute-start.1
  5.4 1.6 %collective-permute-start = (f32[128,128]{1,0:T(8,128)S(1)}, f32[128,128]{1,0:T(8,128)S(1)}, u32[]{:S(2)}, u32[]{:S(2)}) collective-permute-start(f32[128,128]{1,0:T(8,128)S(1)} %get-tuple-element.17.ends), channel_id=1, source_target_pairs={{0,1},{1,0},{2,3},{3,2},{4,5},{5,4},{6,7},{7,6},{8,9},{9,8},{10,11... | collective-permute-start | bytes 196616 | tf_op jit(solution)/shard_map/ppermute | solution.py:487
  7.0 2.1 %collective-permute-done.1.other = f32[128,128]{1,0:T(8,128)S(1)} collective-permute-done((f32[128,128]{1,0:T(8,128)S(1)}, f32[128,128]{1,0:T(8,128)S(1)}, u32[]{:S(2)}, u32[]{:S(2)}) %collective-permute-start.1) | collective-permute-done | bytes 65568 | tf_op jit(solution)/shard_map/ppermute | solution.py:489
  9.1 0.0 collective-permute-done.mate
  9.1 0.4 collective-permute-start.4
  9.6 1.9 %collective-permute-start.6 = (f32[608,128]{1,0:T(8,128)S(1)}, f32[608,128]{1,0:T(8,128)S(1)}, u32[]{:S(2)}, u32[]{:S(2)}) collective-permute-start(f32[608,128]{1,0:T(8,128)S(1)} %get-tuple-element.24), channel_id=1, source_target_pairs={{0,8},{8,16},{16,24},{24,32},{32,40},{40,48},{48,56},{56,0},{1,9},... | collective-permute-start | bytes 933896 | tf_op jit(solution)/shard_map/ppermute | solution.py:472
  11.5 3.9 %collective-permute-start.7 = (f32[608,128]{1,0:T(8,128)S(1)}, f32[608,128]{1,0:T(8,128)S(1)}, u32[]{:S(2)}, u32[]{:S(2)}) collective-permute-start(f32[608,128]{1,0:T(8,128)S(1)} %get-tuple-element.25), channel_id=1, source_target_pairs={{0,56},{8,0},{16,8},{24,16},{32,24},{40,32},{48,40},{56,48},{1,57}... | collective-permute-start | bytes 933896 | tf_op jit(solution)/shard_map/ppermute | solution.py:472
  15.4 0.0 collective-permute-done.4.sprev
  15.5 2.9 %collective-permute-start.5 = (f32[128,128]{1,0:T(8,128)S(1)}, f32[128,128]{1,0:T(8,128)S(1)}, u32[]{:S(2)}, u32[]{:S(2)}) collective-permute-start(f32[128,128]{1,0:T(8,128)S(1)} %get-tuple-element.22), channel_id=1, source_target_pairs={{0,192},{64,0},{128,64},{192,128},{1,193},{65,1},{129,65},{193,129... | collective-permute-start | bytes 196616 | tf_op jit(solution)/shard_map/ppermute | solution.py:472
  18.3 1.9 %collective-permute-done.5.snext = f32[128,128]{1,0:T(8,128)S(1)} collective-permute-done((f32[128,128]{1,0:T(8,128)S(1)}, f32[128,128]{1,0:T(8,128)S(1)}, u32[]{:S(2)}, u32[]{:S(2)}) %collective-permute-start.5) | collective-permute-done | bytes 65568 | tf_op jit(solution)/shard_map/ppermute | solution.py:472
  20.2 0.0 collective-permute-done.2.xprev
  20.2 0.0 collective-permute-done.3.xnext
  20.2 0.1 shard_map.52
  20.4 0.7 %collective-permute-start.8 = (f32[384,128]{1,0:T(8,128)S(1)}, f32[384,128]{1,0:T(8,128)S(1)}, u32[]{:S(2)}, u32[]{:S(2)}) collective-permute-start(f32[384,128]{1,0:T(8,128)S(1)} %get-tuple-element.26), channel_id=1, source_target_pairs={{0,8},{8,16},{16,24},{24,32},{32,40},{40,48},{48,56},{56,0},{1,9},... | collective-permute-start | bytes 589832 | tf_op jit(solution)/shard_map/ppermute | solution.py:472
  21.1 4.2 %collective-permute-start.9 = (f32[384,128]{1,0:T(8,128)S(1)}, f32[384,128]{1,0:T(8,128)S(1)}, u32[]{:S(2)}, u32[]{:S(2)}) collective-permute-start(f32[384,128]{1,0:T(8,128)S(1)} %get-tuple-element.27), channel_id=1, source_target_pairs={{0,56},{8,0},{16,8},{24,16},{32,24},{40,32},{48,40},{56,48},{1,57}... | collective-permute-start | bytes 589832 | tf_op jit(solution)/shard_map/ppermute | solution.py:472
  25.3 0.0 collective-permute-done.6.prev
  25.3 0.0 collective-permute-done.7.nxt
  25.4 3.3 %collective-permute-done.8.eprev = f32[384,128]{1,0:T(8,128)S(1)} collective-permute-done((f32[384,128]{1,0:T(8,128)S(1)}, f32[384,128]{1,0:T(8,128)S(1)}, u32[]{:S(2)}, u32[]{:S(2)}) %collective-permute-start.8) | collective-permute-done | bytes 196640 | tf_op jit(solution)/shard_map/ppermute | solution.py:472
  28.7 0.0 collective-permute-done.9.enext
  28.7 7.5 %shard_map.54 = (f32[5120,128]{1,0:T(8,128)S(1)}, f32[32,128]{1,0:T(8,128)S(1)}) custom-call(f32[1280,128]{1,0:T(8,128)S(1)} %bitcast.5, f32[256,128]{1,0:T(8,128)S(1)} %get-tuple-element.18.slabs, f32[1216,128]{1,0:T(8,128)S(1)} %get-tuple-element.23.kept, f32[128,128]{1,0:T(8,128)S(1)} %collective-permute-done.4.sprev, ...), custom_call_target="tpu_custom_call" | custom-call | tf_op jit(solution)/shard_map/pallas_call | solution.py:460
  36.2 0.1 collective-permute-start.10
  36.3 1.2 %collective-permute-done.10 = f32[32,128]{1,0:T(8,128)S(1)} collective-permute-done((f32[32,128]{1,0:T(8,128)S(1)}, f32[32,128]{1,0:T(8,128)S(1)}, u32[]{:S(2)}, u32[]{:S(2)}) %collective-permute-start.10) | collective-permute-done | bytes 16416 | tf_op jit(solution)/shard_map/ppermute | solution.py:472
  37.5 14.5 %all_to_all.10 = f32[16,32,128]{2,1,0:T(8,128)S(1)} all-to-all(f32[16,32,128]{2,1,0:T(8,128)S(1)} %broadcast_in_dim.7), channel_id=1, replica_groups=mesh['gx'=4,'gy'=8,'zx'=4,'core'=2] {'gx','zx'}, dimensions={0} | all-to-all | bytes 524288 | tf_op jit(solution)/shard_map/all_to_all | solution.py:477
  52.0 14.8 %all_to_all.11.parts = f32[8,32,128]{2,1,0:T(8,128)S(1)} all-to-all(f32[8,32,128]{2,1,0:T(8,128)S(1)} %broadcast_in_dim.8), channel_id=1, replica_groups=mesh['gx'=4,'gy'=8,'zx'=4,'core'=2] {'gy'}, dimensions={0} | all-to-all | bytes 262144 | tf_op jit(solution)/shard_map/all_to_all | solution.py:477
  66.7 4.5 %shard_map.55 = (f32[16,64,128]{2,1,0:T(8,128)}, f32[16,64,128]{2,1,0:T(8,128)}) custom-call(f32[8,32,128]{2,1,0:T(8,128)S(1)} %all_to_all.11.parts, f32[5120,128]{1,0:T(8,128)S(1)} %get-tuple-element.29.basis), custom_call_target="tpu_custom_call" | custom-call | tf_op jit(solution)/shard_map/pallas_call | solution.py:460
  (6 shorter events, 0.1 us)
Async XLA Ops:
  2.1 18.1 %collective-permute-start.2 = (f32[608,128]{1,0:T(8,128)S(1)}, f32[608,128]{1,0:T(8,128)S(1)}, u32[]{:S(2)}, u32[]{:S(2)}) collective-permute-start(f32[608,128]{1,0:T(8,128)S(1)} %get-tuple-element.19), channel_id=1, source_target_pairs={{0,64},{64,128},{128,192},{192,0},{1,65},{65,129},{129,193},{193,1... | collective-permute-start | bytes 933896 | tf_op jit(solution)/shard_map/ppermute | solution.py:472
  3.8 16.5 %collective-permute-start.3 = (f32[608,128]{1,0:T(8,128)S(1)}, f32[608,128]{1,0:T(8,128)S(1)}, u32[]{:S(2)}, u32[]{:S(2)}) collective-permute-start(f32[608,128]{1,0:T(8,128)S(1)} %get-tuple-element.20), channel_id=1, source_target_pairs={{0,192},{64,0},{128,64},{192,128},{1,193},{65,1},{129,65},{193,129... | collective-permute-start | bytes 933896 | tf_op jit(solution)/shard_map/ppermute | solution.py:472
  5.4 3.7 %collective-permute-start.1 = (f32[128,128]{1,0:T(8,128)S(1)}, f32[128,128]{1,0:T(8,128)S(1)}, u32[]{:S(2)}, u32[]{:S(2)}) collective-permute-start(f32[128,128]{1,0:T(8,128)S(1)} %get-tuple-element.17.ends), channel_id=1, source_target_pairs={{1,2},{3,4},{5,6},{7,0},{2,1},{4,3},{6,5},{0,7},{9,10},{11,12},{13... | collective-permute-start | bytes 196616 | tf_op jit(solution)/shard_map/ppermute | solution.py:489
  5.4 3.7 %collective-permute-start = (f32[128,128]{1,0:T(8,128)S(1)}, f32[128,128]{1,0:T(8,128)S(1)}, u32[]{:S(2)}, u32[]{:S(2)}) collective-permute-start(f32[128,128]{1,0:T(8,128)S(1)} %get-tuple-element.17.ends), channel_id=1, source_target_pairs={{0,1},{1,0},{2,3},{3,2},{4,5},{5,4},{6,7},{7,6},{8,9},{9,8},{10,11... | collective-permute-start | bytes 196616 | tf_op jit(solution)/shard_map/ppermute | solution.py:487
  9.1 6.3 %collective-permute-start.4 = (f32[128,128]{1,0:T(8,128)S(1)}, f32[128,128]{1,0:T(8,128)S(1)}, u32[]{:S(2)}, u32[]{:S(2)}) collective-permute-start(f32[128,128]{1,0:T(8,128)S(1)} %get-tuple-element.21), channel_id=1, source_target_pairs={{0,64},{64,128},{128,192},{192,0},{1,65},{65,129},{129,193},{193,1... | collective-permute-start | bytes 196616 | tf_op jit(solution)/shard_map/ppermute | solution.py:472
  9.6 15.7 %collective-permute-start.6 = (f32[608,128]{1,0:T(8,128)S(1)}, f32[608,128]{1,0:T(8,128)S(1)}, u32[]{:S(2)}, u32[]{:S(2)}) collective-permute-start(f32[608,128]{1,0:T(8,128)S(1)} %get-tuple-element.24), channel_id=1, source_target_pairs={{0,8},{8,16},{16,24},{24,32},{32,40},{40,48},{48,56},{56,0},{1,9},... | collective-permute-start | bytes 933896 | tf_op jit(solution)/shard_map/ppermute | solution.py:472
  11.5 13.8 %collective-permute-start.7 = (f32[608,128]{1,0:T(8,128)S(1)}, f32[608,128]{1,0:T(8,128)S(1)}, u32[]{:S(2)}, u32[]{:S(2)}) collective-permute-start(f32[608,128]{1,0:T(8,128)S(1)} %get-tuple-element.25), channel_id=1, source_target_pairs={{0,56},{8,0},{16,8},{24,16},{32,24},{40,32},{48,40},{56,48},{1,57}... | collective-permute-start | bytes 933896 | tf_op jit(solution)/shard_map/ppermute | solution.py:472
  15.5 4.8 %collective-permute-start.5 = (f32[128,128]{1,0:T(8,128)S(1)}, f32[128,128]{1,0:T(8,128)S(1)}, u32[]{:S(2)}, u32[]{:S(2)}) collective-permute-start(f32[128,128]{1,0:T(8,128)S(1)} %get-tuple-element.22), channel_id=1, source_target_pairs={{0,192},{64,0},{128,64},{192,128},{1,193},{65,1},{129,65},{193,129... | collective-permute-start | bytes 196616 | tf_op jit(solution)/shard_map/ppermute | solution.py:472
  20.4 8.3 %collective-permute-start.8 = (f32[384,128]{1,0:T(8,128)S(1)}, f32[384,128]{1,0:T(8,128)S(1)}, u32[]{:S(2)}, u32[]{:S(2)}) collective-permute-start(f32[384,128]{1,0:T(8,128)S(1)} %get-tuple-element.26), channel_id=1, source_target_pairs={{0,8},{8,16},{16,24},{24,32},{32,40},{40,48},{48,56},{56,0},{1,9},... | collective-permute-start | bytes 589832 | tf_op jit(solution)/shard_map/ppermute | solution.py:472
  21.1 7.6 %collective-permute-start.9 = (f32[384,128]{1,0:T(8,128)S(1)}, f32[384,128]{1,0:T(8,128)S(1)}, u32[]{:S(2)}, u32[]{:S(2)}) collective-permute-start(f32[384,128]{1,0:T(8,128)S(1)} %get-tuple-element.27), channel_id=1, source_target_pairs={{0,56},{8,0},{16,8},{24,16},{32,24},{40,32},{48,40},{56,48},{1,57}... | collective-permute-start | bytes 589832 | tf_op jit(solution)/shard_map/ppermute | solution.py:472
  36.2 1.2 %collective-permute-start.10 = (f32[32,128]{1,0:T(8,128)S(1)}, f32[32,128]{1,0:T(8,128)S(1)}, u32[]{:S(2)}, u32[]{:S(2)}) collective-permute-start(f32[32,128]{1,0:T(8,128)S(1)} %get-tuple-element.28), channel_id=1, source_target_pairs={{0,1},{1,0},{2,3},{3,2},{4,5},{5,4},{6,7},{7,6},{8,9},{9,8},{10,11... | collective-permute-start | bytes 49160 | tf_op jit(solution)/shard_map/ppermute | solution.py:472
